TPU v7x, 256 devices: a whole 4x4x8 slice. The times are simulated.
256 devices in a mesh: group: 8 (over y, core), local: 32 (over z, x).
Axes of the slice: x: 4, y: 4, z: 8, core: 2. Of those that a mesh axis runs over, the one named last changes fastest.
Arguments:
- tokens: bfloat16 [6144, 2048], P(('group', 'local')), may hold values from -6 to 6
- out_grad: bfloat16 [6144, 2048], P(('group', 'local')), may hold values from -0.59765625 to 0.59765625
- experts: int32 [6144, 8], P(('group', 'local')), may hold values from 0 to 127, as said below
- gate_values: float32 [6144, 8], P(('group', 'local')), may hold values from 0.02 to 0.5
- slot_map: int32 [8, 32], replicated, may hold values from 0 to 31, each once within a row
- gate_weight: bfloat16 [256, 2048, 384], P(('group', 'local')), may hold values from -0.125 to 0.125
- up_weight: bfloat16 [256, 2048, 384], P(('group', 'local')), may hold values from -0.125 to 0.125
- down_weight: bfloat16 [256, 384, 2048], P(('group', 'local')), may hold values from -0.21875 to 0.21875
Outputs:
- layer_out: bfloat16 [6144, 2048], P(('group', 'local'))
- token_grad: bfloat16 [6144, 2048], P(('group', 'local'))
- gate_grad: float32 [6144, 8], P(('group', 'local'))
- gate_weight_grad: bfloat16 [256, 2048, 384], P(('group', 'local'))
- up_weight_grad: bfloat16 [256, 2048, 384], P(('group', 'local'))
- down_weight_grad: bfloat16 [256, 384, 2048], P(('group', 'local'))
Inputs may be any that keep to these rules, and one draw needn't show every extreme that they name: A token names 8 different experts, all within at most 4 groups of 16 consecutive experts; the tokens of one device name each expert at most 3 times, and in every draw some expert is named exactly 3 times by the tokens of every device. `slot_map`: each row is a permutation; in group g the two devices whose entries are 2 k and 2 k + 1 hold expert g * 16 + k.
All inputs are finite; a program needn't handle non-finite values.
Results may differ from a plain program's by a relative error of at most 0.0064.
Values may be sent and summed in bfloat16 or wider, within the bound.
No kernel may reach another device: no remote copies, remote signals or barrier semaphores. Data moves between devices by JAX's collectives and lax.ppermute only.
A program may use at most 128 MiB of HBM per device.

v0:
```python
import functools

import jax
import jax.numpy as jnp
from jax import lax
from jax.experimental import pallas as pl
from jax.experimental.pallas import tpu as pltpu
from jax.sharding import Mesh
from jax.sharding import PartitionSpec as P

BF = jnp.bfloat16
F32 = jnp.float32
SPREAD = ("y", "core", "zlo", "x")
EXTRA = 128
SORT = 8
STEPS = (0, 1, 2, 3)
INNER = (((0,), (0,)), ((), ()))
OUTER = (((1,), (1,)), ((), ()))
VMEM_LIMIT = 48 * 1024 * 1024


def iota(shape, dim):
    return lax.broadcasted_iota(jnp.int32, shape, dim)


def identity(n):
    return (iota((n, n), 0) == iota((n, n), 1)).astype(BF)


def whole(a):
    return pl.BlockSpec(a.shape, lambda i: (0, 0))


def cost(flops, moved, special=0):
    return pl.CostEstimate(flops=flops, bytes_accessed=moved, transcendentals=special)


def params():
    return pltpu.CompilerParams(vmem_limit_bytes=VMEM_LIMIT)


def make_tables(here, top, slots, info, dest_expert, code_ref, weight_ref, ids_ref):
    dests, held = code_ref.shape
    info_t = lax.dot_general(identity(EXTRA), info, OUTER, preferred_element_type=F32)
    ids = info_t[:top]
    gates = info_t[top : 2 * top] + info_t[2 * top : 3 * top] + info_t[3 * top : 4 * top]
    names = jnp.zeros((dests, held), F32)
    weight = jnp.zeros((dests, held), F32)
    for j in range(top):
        matched = ids[j : j + 1] == dest_expert
        names += jnp.where(matched, 1.0, 0.0)
        weight += jnp.where(matched, gates[j : j + 1], 0.0)
    first, later = iota((held, held), 0), iota((held, held), 1)
    before = ((first // here == later // here) & (first < later)).astype(BF)
    rank = jnp.dot(names.astype(BF), before, preferred_element_type=F32)
    row = iota((dests, held), 1)
    blocks = held // (2 * here)
    place = row // (2 * here) + row // here % 2 * (slots // 2)
    code_ref[...] = jnp.where(names > 0.0, rank * float(blocks) + place.astype(F32), -1.0)
    weight_ref[...] = weight
    ids_ref[...] = ids


def pack_kernel(tokens_ref, out_grad_ref, experts_ref, gates_ref, out_ref):
    here, width = tokens_ref.shape
    top = experts_ref.shape[0]
    gates = gates_ref[...]
    high = gates.astype(BF)
    middle = (gates - high.astype(F32)).astype(BF)
    low = (gates - high.astype(F32) - middle.astype(F32)).astype(BF)
    extra = jnp.zeros((here, EXTRA), F32)
    for k, part in enumerate((experts_ref[...].astype(F32).astype(BF), high, middle, low)):
        place = (iota((top, EXTRA), 0) + k * top == iota((top, EXTRA), 1)).astype(BF)
        extra += lax.dot_general(part, place, INNER, preferred_element_type=F32)
    rows = [tokens_ref[...].astype(F32), out_grad_ref[...].astype(F32)]
    out_ref[:, :width] = jnp.concatenate(rows, axis=0).astype(BF)
    out_ref[:, width:] = jnp.concatenate([extra, extra], axis=0).astype(BF)


def pack(tokens, out_grad, experts_t, gates_t):
    here, width = tokens.shape
    return pl.pallas_call(
        pack_kernel,
        out_shape=jax.ShapeDtypeStruct((2 * here, width + EXTRA), BF),
        name="pack",
    )(tokens, out_grad, experts_t, gates_t)


def fill_kernel(here, top, slots, rows_ref, expert_ref, out_ref, code_ref, weight_ref, ids_ref):
    held, width = rows_ref.shape[0], out_ref.shape[1]
    step = pl.program_id(0)

    @pl.when(step == 0)
    def _():
        make_tables(here, top, slots, rows_ref[:, width:], expert_ref[...][:, :1], code_ref, weight_ref, ids_ref)

    part = out_ref.shape[0] // slots
    at = pl.ds(pl.multiple_of(step * part, part), part)
    chosen = code_ref[at, :][:, None, :] == iota((part, slots, held), 1).astype(F32)
    scale = jnp.where(iota((part, held), 1) // here % 2 == 0, 1.0, weight_ref[at, :])
    scaled = jnp.where(chosen, scale[:, None, :], 0.0).reshape(part * slots, held)
    scale = jnp.sum(scaled, axis=1, keepdims=True)
    mask = jnp.where(chosen, 1.0, 0.0).reshape(part * slots, held).astype(BF)
    raw = jnp.dot(mask, rows_ref[:, :width], preferred_element_type=F32)
    out_ref[...] = (scale * raw).astype(BF)


def fill(rows, dest_expert, here, top, slots, width, steps=4):
    held = rows.shape[0]
    dests = dest_expert.shape[0]
    part = dests // steps * slots
    tables = [(dests, held), (dests, held), (top, held)]
    return pl.pallas_call(
        functools.partial(fill_kernel, here, top, slots),
        grid=(steps,),
        in_specs=[whole(rows), whole(dest_expert)],
        out_specs=[pl.BlockSpec((part, width), lambda i: (i, 0))]
        + [pl.BlockSpec(shape, lambda i: (0, 0)) for shape in tables],
        out_shape=[jax.ShapeDtypeStruct((dests * slots, width), BF)]
        + [jax.ShapeDtypeStruct(shape, F32) for shape in tables],
        compiler_params=params(),
        cost_estimate=cost(2 * dests * slots * held * width, 2 * dests * slots * width),
        name="fill",
    )(rows, dest_expert)


def sorting(slots, transposed=False):
    half, count = slots // 2, SORT * slots
    a, b = iota((count, count), 0), iota((count, count), 1)
    if transposed:
        a, b = b, a
    kind, place = a // (SORT * half), a % (SORT * half)
    return (place // half * slots + kind * half + place % half == b).astype(BF)


def sort_rows(order, rows):
    return jnp.dot(order, rows, preferred_element_type=F32).astype(BF)


def kind_rows(kind, slots, rows_ref):
    count = SORT * slots
    half = count // 2
    place, at = iota((half, count), 0), iota((half, count), 1)
    order = (place // (slots // 2) * slots + kind * (slots // 2) + place % (slots // 2) == at).astype(BF)
    parts = [sort_rows(order, rows_ref[i : i + count, :]) for i in range(0, rows_ref.shape[0], count)]
    return jnp.concatenate(parts, axis=0)


def split_rows(slots, rows, out_ref):
    order = sorting(slots, transposed=True)
    count = order.shape[0]
    half, features = count // 2, rows.shape[1] // 2
    for i in range(rows.shape[0] // half):
        part = rows[i * half : (i + 1) * half]
        both = jnp.concatenate([part[:, :features], part[:, features:]], axis=0)
        out_ref[i * count : (i + 1) * count, :] = sort_rows(order, both)


def forward_kernel(slots, rows_ref, gate_ref, up_ref, down_ref, out_ref, hidden_ref, active_ref, slope_ref):
    slot_rows = kind_rows(0, slots, rows_ref)
    gate_pre = jnp.dot(slot_rows, gate_ref[...], preferred_element_type=F32)
    up_pre = jnp.dot(slot_rows, up_ref[...], preferred_element_type=F32)
    sigmoid_gate = jax.nn.sigmoid(gate_pre)
    active = gate_pre * sigmoid_gate
    hidden = (active * up_pre).astype(BF)
    hidden_ref[...] = hidden
    active_ref[...] = active
    slope_ref[...] = up_pre * sigmoid_gate * (1.0 + gate_pre * (1.0 - sigmoid_gate))
    partial_rows = jnp.dot(hidden, down_ref[...], preferred_element_type=F32).astype(BF)
    split_rows(slots, partial_rows, out_ref)


def backward_kernel(slots, rows_ref, active_ref, slope_ref, gate_ref, up_ref, down_ref,
                    out_ref, gate_grad_ref, up_grad_ref):
    scaled = kind_rows(1, slots, rows_ref)
    hidden_grad = lax.dot_general(scaled, down_ref[...], OUTER, preferred_element_type=F32)
    gate_pre_grad = (hidden_grad * slope_ref[...]).astype(BF)
    up_pre_grad = (hidden_grad * active_ref[...]).astype(BF)
    gate_grad_ref[...] = gate_pre_grad
    up_grad_ref[...] = up_pre_grad
    back_rows = (
        lax.dot_general(gate_pre_grad, gate_ref[...], OUTER, preferred_element_type=F32)
        + lax.dot_general(up_pre_grad, up_ref[...], OUTER, preferred_element_type=F32)
    ).astype(BF)
    split_rows(slots, back_rows, out_ref)


def expert_call(kernel, rows, kept, slabs, outs, name, slots, steps=4):
    count, width = rows.shape
    units = slabs[0].shape[1]
    chunk = lambda size, columns: pl.BlockSpec((size // steps, columns), lambda i: (i, 0))
    return pl.pallas_call(
        functools.partial(kernel, slots),
        grid=(steps,),
        in_specs=[chunk(count, width)] + [chunk(count // 2, units)] * len(kept) + [whole(a) for a in slabs],
        out_specs=[chunk(count, width // 2)] + [chunk(count // 2, units)] * len(outs),
        out_shape=[jax.ShapeDtypeStruct((count, width // 2), BF)]
        + [jax.ShapeDtypeStruct((count // 2, units), kind) for kind in outs],
        compiler_params=params(),
        cost_estimate=cost(3 * count * units * width, 3 * count * width + 6 * units * width, count * units),
        name=name,
    )(rows, *kept, *slabs)


def slab_grad_kernel(slots, rows_ref, hidden_ref, gate_grad_ref, up_grad_ref, gate_out, up_out, down_out, token_ref, grad_ref):
    count = SORT * slots
    half = count // 2
    order = sorting(slots)
    for i in range(rows_ref.shape[0] // count):
        rows = sort_rows(order, rows_ref[i * count : (i + 1) * count, :])
        token_ref[i * half : (i + 1) * half, :] = rows[:half]
        grad_ref[i * half : (i + 1) * half, :] = rows[half:]
    slot_rows = token_ref[...]
    gate_out[...] = lax.dot_general(slot_rows, gate_grad_ref[...], INNER, preferred_element_type=F32).astype(BF)
    up_out[...] = lax.dot_general(slot_rows, up_grad_ref[...], INNER, preferred_element_type=F32).astype(BF)
    down_out[...] = lax.dot_general(hidden_ref[...], grad_ref[...], INNER, preferred_element_type=F32).astype(BF)


def slab_grads(rows, hidden, gate_pre_grad, up_pre_grad, slots, steps=4):
    count, width = rows.shape
    units = hidden.shape[1]
    part = width // steps
    return pl.pallas_call(
        functools.partial(slab_grad_kernel, slots),
        grid=(steps,),
        in_specs=[pl.BlockSpec((count, part), lambda i: (0, i)), whole(hidden), whole(hidden), whole(hidden)],
        out_specs=[pl.BlockSpec((part, units), lambda i: (i, 0))] * 2
        + [pl.BlockSpec((units, part), lambda i: (0, i))],
        out_shape=[jax.ShapeDtypeStruct((width, units), BF)] * 2 + [jax.ShapeDtypeStruct((units, width), BF)],
        scratch_shapes=[pltpu.VMEM((count // 2, part), BF)] * 2,
        compiler_params=params(),
        cost_estimate=cost(3 * count * units * width, 2 * count * width + 6 * units * width),
        name="slab_grads",
    )(rows, hidden, gate_pre_grad, up_pre_grad)


def by_row(table, slots, count):
    repeat = (iota((table.shape[0], count), 1) // slots == iota((table.shape[0], count), 0)).astype(BF)
    return lax.dot_general(table.astype(BF), repeat, INNER, preferred_element_type=F32)


def prepare_kernel(here, slots, rows_ref, code_ref, weight_ref, high_ref, low_ref, mask_ref, grad_ref):
    held, count = high_ref.shape
    half = grad_ref.shape[1]
    slot = (iota((held, count), 1) % slots).astype(F32)
    chosen = by_row(code_ref[...], slots, count) == slot
    weight = weight_ref[...]
    high = weight.astype(BF).astype(F32)
    mask_ref[...] = jnp.where(chosen, 1.0, 0.0).astype(BF)
    high_ref[...] = jnp.where(chosen, by_row(high, slots, count), 0.0).astype(BF)
    low_ref[...] = jnp.where(chosen, by_row(weight - high, slots, count), 0.0).astype(BF)
    for k in range(0, held, 2 * here):
        rows = rows_ref[k : k + 2 * here, : 2 * half].astype(F32)[here:]
        grad_ref[k : k + 2 * here, :] = jnp.concatenate([rows[:, :half], rows[:, half:]], axis=0).astype(BF)


def prepare(rows, code, weight, here, slots):
    held, wide = rows.shape
    count = code.shape[0] * slots
    return pl.pallas_call(
        functools.partial(prepare_kernel, here, slots),
        out_shape=[jax.ShapeDtypeStruct((held, count), BF)] * 3
        + [jax.ShapeDtypeStruct((held, (wide - EXTRA) // 2), BF)],
        compiler_params=params(),
        name="prepare",
    )(rows, code, weight)


def store_blocks(index_ref, total_ref, outs, columns):
    size = outs[0].shape[0]
    for k, out_ref in zip(STEPS, outs):
        at = pl.multiple_of((index_ref[0, 0] + k) % len(outs) * size, size)
        out_ref[:, columns] = total_ref[pl.ds(at, size), :].astype(BF)


def layer_sum_kernel(slots, index_ref, back_ref, rows_ref, code_ref, ids_ref, expert_ref, high_ref, low_ref, *refs):
    *outs, total_ref, gate_ref, dots_ref = refs
    held = high_ref.shape[0]
    top = ids_ref.shape[0]
    dests = code_ref.shape[0]
    part = back_ref.shape[1]
    half = outs[0].shape[1] - EXTRA
    step = pl.program_id(0)

    @pl.when(step == 0)
    def _():
        dots_ref[...] = jnp.zeros_like(dots_ref)

    back = back_ref[...]
    total_ref[...] = jnp.dot(high_ref[...], back, preferred_element_type=F32) + jnp.dot(
        low_ref[...], back, preferred_element_type=F32
    )
    store_blocks(index_ref, total_ref, outs, pl.ds(pl.multiple_of(step * part, part), part))
    dots_ref[...] += lax.dot_general(back, rows_ref[...], OUTER, preferred_element_type=F32)

    @pl.when(step == pl.num_programs(0) - 1)
    def _():
        chosen = code_ref[...][:, None, :] == iota((dests, slots, held), 1).astype(F32)
        by_dest = jnp.sum(jnp.where(chosen, dots_ref[...].reshape(dests, slots, held), 0.0), axis=1)
        dest_expert = expert_ref[...][:, :1]
        rows = [
            jnp.sum(jnp.where(ids_ref[j : j + 1, :] == dest_expert, by_dest, 0.0), axis=0, keepdims=True)
            for j in range(top)
        ]
        gate = jnp.concatenate(rows + [jnp.zeros((EXTRA - top, held), F32)], axis=0)
        gate_ref[...] = lax.dot_general(gate.astype(BF), identity(EXTRA), INNER, preferred_element_type=F32)
        store_blocks(index_ref, gate_ref, outs, slice(half, half + EXTRA))


def layer_sums(index, returned, rows, code, ids, dest_expert, high, low, slots, steps=2):
    count, half = returned.shape
    held = rows.shape[0]
    size = held // len(STEPS)
    part = half // steps
    chunk = lambda size: pl.BlockSpec((size, part), lambda i: (0, i))
    return pl.pallas_call(
        functools.partial(layer_sum_kernel, slots),
        grid=(steps,),
        in_specs=[pl.BlockSpec(memory_space=pltpu.SMEM), chunk(count), chunk(held)]
        + [whole(a) for a in (code, ids, dest_expert, high, low)],
        out_specs=[pl.BlockSpec((size, half + EXTRA), lambda i: (0, 0))] * len(STEPS),
        out_shape=[jax.ShapeDtypeStruct((size, half + EXTRA), BF)] * len(STEPS),
        scratch_shapes=[
            pltpu.VMEM((held, part), F32),
            pltpu.VMEM((held, EXTRA), F32),
            pltpu.VMEM((count, held), F32),
        ],
        compiler_params=params(),
        cost_estimate=cost(6 * count * held * half, 2 * count * half),
        name="layer_sums",
    )(index, returned, rows, code, ids, dest_expert, high, low)


def token_sum_kernel(index_ref, back_ref, mask_ref, *refs):
    *outs, total_ref = refs
    total_ref[...] = jnp.dot(mask_ref[...], back_ref[...], preferred_element_type=F32)
    store_blocks(index_ref, total_ref, outs, slice(None))


def token_sums(index, returned, mask, steps=2):
    count, half = returned.shape
    held = mask.shape[0]
    size = held // len(STEPS)
    part = half // steps
    chunk = lambda size: pl.BlockSpec((size, part), lambda i: (0, i))
    return pl.pallas_call(
        token_sum_kernel,
        grid=(steps,),
        in_specs=[pl.BlockSpec(memory_space=pltpu.SMEM), chunk(count), whole(mask)],
        out_specs=[chunk(size)] * len(STEPS),
        out_shape=[jax.ShapeDtypeStruct((size, half), BF)] * len(STEPS),
        scratch_shapes=[pltpu.VMEM((held, part), F32)],
        compiler_params=params(),
        cost_estimate=cost(2 * count * held * half, 2 * count * half),
        name="token_sums",
    )(index, returned, mask)


def sum_blocks(sums):
    n = lax.axis_size("zhi")
    total = sums[0].astype(F32)
    for rows, step in zip(sums[1:], STEPS[1:]):
        moved = lax.ppermute(rows, "zhi", [(i, (i + step) % n) for i in range(n)])
        total += moved.astype(F32)
    return total


def body(tokens, out_grad, experts, gate_values, slot_map, gate_weight, up_weight, down_weight):
    here, width = tokens.shape
    top = experts.shape[1]
    groups, members = slot_map.shape
    blocks = len(STEPS)
    near = members // blocks
    per_group = members // 2
    capacity = 2 * here * top // (groups * per_group)
    dests = groups * near
    slots = 2 * blocks * capacity

    own = pack(tokens, out_grad, experts.T, gate_values.T)
    rows = lax.all_gather(own, "zhi", axis=0, tiled=True)

    column = lax.dynamic_slice_in_dim(slot_map, lax.axis_index("zhi") * near, near, axis=1)
    dest_expert = column // 2 + jnp.arange(groups, dtype=jnp.int32)[:, None] * per_group
    dest_expert = jnp.broadcast_to(dest_expert.reshape(dests, 1).astype(F32), (dests, 128))

    def exchange(rows):
        columns = rows.shape[1]
        moved = lax.all_to_all(
            rows.reshape(dests, slots, columns), SPREAD, split_axis=0, concat_axis=0, tiled=True
        )
        return moved.reshape(dests * slots, columns)

    after = lax.optimization_barrier
    index = lax.axis_index("zhi").astype(jnp.int32).reshape(1, 1)
    slabs = (gate_weight[0], up_weight[0], down_weight[0])
    sent, code, weight, ids = fill(rows, dest_expert, here, top, slots, width)
    arrived = exchange(sent)
    partial_out, hidden, active, slope = expert_call(
        forward_kernel, arrived, (), slabs, (BF, F32, F32), "forward", slots
    )
    partial_out, arrived, rows = after((partial_out, arrived, rows))
    partial_back = exchange(partial_out)
    back_rows, gate_pre_grad, up_pre_grad = expert_call(
        backward_kernel, arrived, (active, slope), slabs, (BF, BF), "backward", slots
    )
    grad_gate, grad_up, grad_down = slab_grads(arrived, hidden, gate_pre_grad, up_pre_grad, slots)
    high, low, mask, grads = prepare(rows, code, weight, here, slots)
    back_rows, partial_back, high, low, mask, grads, grad_gate, grad_up, grad_down = after(
        (back_rows, partial_back, high, low, mask, grads, grad_gate, grad_up, grad_down)
    )
    back_back = exchange(back_rows)
    layer = sum_blocks(layer_sums(index, partial_back, grads, code, ids, dest_expert, high, low, slots))
    back_back, layer = after((back_back, layer))
    token = sum_blocks(token_sums(index, back_back, mask))

    half = width // 2
    layer_out = jnp.concatenate([layer[:here, :half], layer[here:, :half]], axis=1).astype(BF)
    gate_grad = layer[:here, half : half + top] + layer[here:, half : half + top]
    token_grad = jnp.concatenate([token[:here], token[here:]], axis=1).astype(BF)
    return (layer_out, token_grad, gate_grad, grad_gate[None], grad_up[None], grad_down[None])


def solution(mesh):
    groups, members = mesh.devices.shape
    axes = ("y", "core", "zhi", "zlo", "x")
    fine = Mesh(mesh.devices.reshape(groups // 2, 2, members // 8, 2, 4), axes)
    two, three = P(axes, None), P(axes, None, None)
    return jax.shard_map(
        body,
        mesh=fine,
        in_specs=(two, two, two, two, P(), three, three, three),
        out_specs=(two, two, two, three, three, three),
        check_vma=False,
    )
```

profile of v0, /device:TPU:1, one launch (start us, length us, event | category | flops | bytes accessed | tf_op | source)
XLA Modules:
  0.0 247.5 jit_solution(10055086349286114235)
XLA Ops:
  0.7 0.8 fusion.2
  1.4 0.1 convert_element_type.38
  1.5 1.8 pack.1
  3.3 22.2 %all_gather.3.rows_ref = bf16[192,2176]{1,0:T(8,128)(2,1)S(1)} all-gather(bf16[48,2176]{1,0:T(8,128)(2,1)} %pack.1), channel_id=1, replica_groups=mesh['y'=4,'core'=2,'zhi'=4,'zlo'=2,'x'=4] {'zhi'}, dimensions={0}, use_global_device_ids=true | all-gather | bytes 1044480 | tf_op jit(solution)/shard_map/all_gather | solution.py:380
  25.6 0.1 broadcast_in_dim.15.expert_ref
  25.6 4.6 %fill.1 = (bf16[1536,2048]{1,0:T(8,128)(2,1)}, f32[64,192]{1,0:T(8,128)S(1)}, f32[64,192]{1,0:T(8,128)S(1)}, f32[8,192]{1,0:T(8,128)S(1)}) custom-call(bf16[192,2176]{1,0:T(8,128)(2,1)S(1)} %all_gather.3.rows_ref, f32[64,128]{1,0:T(8,128)S(1)} %broadcast_in_dim.15.expert_ref), custom_call_target="tpu_custom_call" | custom-call | flops 1207959552 | bytes 6291456 | tf_op jit(solution)/shard_map/fill/pallas_call | solution.py:113
  30.2 85.7 %all_to_all.15 = bf16[64,24,2048]{2,1,0:T(8,128)(2,1)} all-to-all(bf16[64,24,2048]{2,1,0:T(8,128)(2,1)} %bitcast.23), channel_id=1, replica_groups=mesh['y'=4,'core'=2,'zhi'=4,'zlo'=2,'x'=4] {'y','core','zlo','x'}, dimensions={0} | all-to-all | bytes 12582912 | tf_op jit(solution)/shard_map/all_to_all | solution.py:388
  115.9 0.0 copy-done.2
  115.9 10.9 %forward.1 = (bf16[1536,1024]{1,0:T(8,128)(2,1)}, bf16[768,384]{1,0:T(8,128)(2,1)S(1)}, f32[768,384]{1,0:T(8,128)S(1)}, f32[768,384]{1,0:T(8,128)S(1)}) custom-call(bf16[1536,2048]{1,0:T(8,128)(2,1)} %bitcast.20, bf16[2048,384]{1,0:T(8,128)(2,1)S(1)} %bitcast.16, bf16[2048,384]{1,0:T(8,128)(2,1)S(1)} %bitcast.19, bf16[384,2048]{1,0:T(8,128)(2,1)} %bitcast.28), custom_call_target="tpu_custom_call" | custom-call | flops 3623878656 | bytes 14155776 | tf_op jit(solution)/shard_map/forward/pallas_call | solution.py:192
  126.8 1.0 copy-done.10
  127.8 1.0 copy-done.12
  128.9 0.8 copy-done.14
  129.7 5.6 %all-to-all-start.1 = ((bf16[64,24,1024]{2,1,0:T(8,128)(2,1)}), bf16[64,24,1024]{2,1,0:T(8,128)(2,1)}, u32[]{:S(2)}, u32[]{:S(2)}) async-start(bf16[64,24,1024]{2,1,0:T(8,128)(2,1)} %bitcast.25), calls=%async_computation.1 | async-start | bytes 6291456 | tf_op jit(solution)/shard_map/all_to_all | solution.py:388
  135.3 0.7 prepare.1
  136.0 0.8 copy-done
  136.8 1.8 copy-done.11
  138.7 1.3 copy-done.13
  139.9 13.9 %backward.1 = (bf16[1536,1024]{1,0:T(8,128)(2,1)}, bf16[768,384]{1,0:T(8,128)(2,1)S(1)}, bf16[768,384]{1,0:T(8,128)(2,1)S(1)}) custom-call(bf16[1536,2048]{1,0:T(8,128)(2,1)} %bitcast.21, f32[768,384]{1,0:T(8,128)S(1)} %copy-done.11, f32[768,384]{1,0:T(8,128)S(1)} %copy-done.13, bf16[2048,384]{1,0:T(8,128)(2,1)S(1)} %bitcast.17, bf16[2048,384]{1,0:T(8,128)(2,1)} %bitcast.18, ...), custom_call_target="tpu_custom_call" | custom-call | flops 3623878656 | bytes 14155776 | tf_op jit(solution)/shard_map/backward/pallas_call | solution.py:192
  153.8 0.0 copy-done.8
  153.8 9.3 %slab_grads.1 = (bf16[2048,384]{1,0:T(8,128)(2,1)}, bf16[2048,384]{1,0:T(8,128)(2,1)}, bf16[384,2048]{1,0:T(8,128)(2,1)}) custom-call(bf16[1536,2048]{1,0:T(8,128)(2,1)} %bitcast.22, bf16[768,384]{1,0:T(8,128)(2,1)S(1)} %copy-done.15, bf16[768,384]{1,0:T(8,128)(2,1)S(1)} %get-tuple-element.61.gate_grad_ref, bf16[768,384]{1,0:T(8,128)(2,1)S(1)} %get-tuple-element.62.up_grad_ref), custom_call_target="tpu_custom_call" | custom-call | flops 3623878656 | bytes 11010048 | tf_op jit(solution)/shard_map/slab_grads/pallas_call | solution.py:223
  163.1 13.0 %all-to-all-done.1 = bf16[64,24,1024]{2,1,0:T(8,128)(2,1)} async-done(((bf16[64,24,1024]{2,1,0:T(8,128)(2,1)}), bf16[64,24,1024]{2,1,0:T(8,128)(2,1)}, u32[]{:S(2)}, u32[]{:S(2)}) %all-to-all-start.1) | async-done | bytes 3145760 | tf_op jit(solution)/shard_map/all_to_all | solution.py:388
  176.1 5.1 %all-to-all-start.2 = ((bf16[64,24,1024]{2,1,0:T(8,128)(2,1)}), bf16[64,24,1024]{2,1,0:T(8,128)(2,1)S(1)}, u32[]{:S(2)}, u32[]{:S(2)}) async-start(bf16[64,24,1024]{2,1,0:T(8,128)(2,1)} %bitcast.24), calls=%async_computation.2 | async-start | bytes 6291456 | tf_op jit(solution)/shard_map/all_to_all | solution.py:388
  181.2 1.1 copy-done.5
  182.3 1.1 copy-done.7
  183.3 1.0 copy-done.9
  184.3 4.6 %layer_sums.1 = (bf16[48,1152]{1,0:T(8,128)(2,1)S(1)}, bf16[48,1152]{1,0:T(8,128)(2,1)S(1)}, bf16[48,1152]{1,0:T(8,128)(2,1)S(1)}, bf16[48,1152]{1,0:T(8,128)(2,1)S(1)}) custom-call(s32[1,1]{1,0:T(1,128)} %bitcast.11.index_ref, bf16[1536,1024]{1,0:T(8,128)(2,1)} %bitcast.8.back_ref, bf16[192,1024]{1,0:T(8,128)(2,1)S(1)} %copy-done.9, ...), custom_call_target="tpu_custom_call" | custom-call | flops 1811939328 | bytes 3145728 | tf_op jit(solution)/shard_map/layer_sums/pallas_call | solution.py:316
  188.9 1.0 collective-permute-start
  189.9 2.1 collective-permute-start.1
  192.0 3.4 %collective-permute-start.2 = (bf16[48,1152]{1,0:T(8,128)(2,1)S(1)}, bf16[48,1152]{1,0:T(8,128)(2,1)S(1)}, u32[]{:S(2)}, u32[]{:S(2)}) collective-permute-start(bf16[48,1152]{1,0:T(8,128)(2,1)S(1)} %get-tuple-element.75), channel_id=1, source_target_pairs={{0,24},{8,0},{16,8},{24,16},{1,25},{9,1},{17,9},{25,17},{2,26},{10... | collective-permute-start | bytes 331784 | tf_op jit(solution)/shard_map/ppermute | solution.py:363
  195.4 26.0 %collective-permute-done = bf16[48,1152]{1,0:T(8,128)(2,1)S(1)} collective-permute-done((bf16[48,1152]{1,0:T(8,128)(2,1)S(1)}, bf16[48,1152]{1,0:T(8,128)(2,1)S(1)}, u32[]{:S(2)}, u32[]{:S(2)}) %collective-permute-start) | collective-permute-done | bytes 110624 | tf_op jit(solution)/shard_map/ppermute | solution.py:363
  221.4 6.8 %collective-permute-done.1 = bf16[48,1152]{1,0:T(8,128)(2,1)S(1)} collective-permute-done((bf16[48,1152]{1,0:T(8,128)(2,1)S(1)}, bf16[48,1152]{1,0:T(8,128)(2,1)S(1)}, u32[]{:S(2)}, u32[]{:S(2)}) %collective-permute-start.1) | collective-permute-done | bytes 110624 | tf_op jit(solution)/shard_map/ppermute | solution.py:363
  228.2 0.0 collective-permute-done.2
  228.2 0.1 convert_add_fusion
  228.3 0.0 all-to-all-done.2
  228.3 0.6 copy-done.16
  229.0 0.7 fusion.4
  229.6 1.1 copy-done.1
  230.7 1.3 token_sums.1
  232.0 0.1 collective-permute-start.3
  232.1 2.8 %collective-permute-start.4 = (bf16[48,1024]{1,0:T(8,128)(2,1)S(1)}, bf16[48,1024]{1,0:T(8,128)(2,1)S(1)}, u32[]{:S(2)}, u32[]{:S(2)}) collective-permute-start(bf16[48,1024]{1,0:T(8,128)(2,1)S(1)} %get-tuple-element.81), channel_id=1, source_target_pairs={{0,16},{8,24},{16,0},{24,8},{1,17},{9,25},{17,1},{25,9},{2,18},{10... | collective-permute-start | bytes 294920 | tf_op jit(solution)/shard_map/ppermute | solution.py:363
  234.9 3.5 %collective-permute-start.5 = (bf16[48,1024]{1,0:T(8,128)(2,1)S(1)}, bf16[48,1024]{1,0:T(8,128)(2,1)S(1)}, u32[]{:S(2)}, u32[]{:S(2)}) collective-permute-start(bf16[48,1024]{1,0:T(8,128)(2,1)S(1)} %get-tuple-element.82), channel_id=1, source_target_pairs={{0,24},{8,0},{16,8},{24,16},{1,25},{9,1},{17,9},{25,17},{2,26},{10... | collective-permute-start | bytes 294920 | tf_op jit(solution)/shard_map/ppermute | solution.py:363
  238.4 0.7 slice_add_fusion
  239.1 0.7 copy.14
  239.7 2.9 %collective-permute-done.3 = bf16[48,1024]{1,0:T(8,128)(2,1)S(1)} collective-permute-done((bf16[48,1024]{1,0:T(8,128)(2,1)S(1)}, bf16[48,1024]{1,0:T(8,128)(2,1)S(1)}, u32[]{:S(2)}, u32[]{:S(2)}) %collective-permute-start.3) | collective-permute-done | bytes 98336 | tf_op jit(solution)/shard_map/ppermute | solution.py:363
  242.6 0.0 collective-permute-done.4
  242.6 3.3 %collective-permute-done.5 = bf16[48,1024]{1,0:T(8,128)(2,1)S(1)} collective-permute-done((bf16[48,1024]{1,0:T(8,128)(2,1)S(1)}, bf16[48,1024]{1,0:T(8,128)(2,1)S(1)}, u32[]{:S(2)}, u32[]{:S(2)}) %collective-permute-start.5) | collective-permute-done | bytes 98336 | tf_op jit(solution)/shard_map/ppermute | solution.py:363
  245.9 0.1 add_convert_fusion
  246.0 1.5 pad_maximum_fusion
  (24 shorter events, 0.1 us)
Async XLA Ops:
  30.2 85.7 %copy-start.2 = (bf16[1,2048,384]{2,1,0:T(8,128)(2,1)S(1)}, bf16[1,2048,384]{2,1,0:T(8,128)(2,1)}, u32[]{:S(2)}) copy-start(bf16[1,2048,384]{2,1,0:T(8,128)(2,1)} %param.13) | copy-start | bytes 4718596
  30.2 85.7 %copy-start.3 = (bf16[1,2048,384]{2,1,0:T(8,128)(2,1)S(1)}, bf16[1,2048,384]{2,1,0:T(8,128)(2,1)}, u32[]{:S(2)}) copy-start(bf16[1,2048,384]{2,1,0:T(8,128)(2,1)} %param.14) | copy-start | bytes 4718596
  126.8 1.0 copy-start.10
  127.8 1.0 copy-start.12
  128.9 0.8 copy-start.14
  129.7 46.4 %all-to-all-start.1 = ((bf16[64,24,1024]{2,1,0:T(8,128)(2,1)}), bf16[64,24,1024]{2,1,0:T(8,128)(2,1)}, u32[]{:S(2)}, u32[]{:S(2)}) async-start(bf16[64,24,1024]{2,1,0:T(8,128)(2,1)} %bitcast.25), calls=%async_computation.1 | async-start | bytes 6291456 | tf_op jit(solution)/shard_map/all_to_all | solution.py:388
  136.0 0.8 copy-start
  136.8 17.0 %copy-start.4 = (bf16[192,1536]{1,0:T(8,128)(2,1)}, bf16[192,1536]{1,0:T(8,128)(2,1)S(1)}, u32[]{:S(2)}) copy-start(bf16[192,1536]{1,0:T(8,128)(2,1)S(1)} %get-tuple-element.70.high_ref) | copy-start | bytes 1769476
  136.8 17.0 %copy-start.6 = (bf16[192,1536]{1,0:T(8,128)(2,1)}, bf16[192,1536]{1,0:T(8,128)(2,1)S(1)}, u32[]{:S(2)}) copy-start(bf16[192,1536]{1,0:T(8,128)(2,1)S(1)} %get-tuple-element.71.low_ref) | copy-start | bytes 1769476
  136.8 17.0 %copy-start.8 = (bf16[192,1024]{1,0:T(8,128)(2,1)}, bf16[192,1024]{1,0:T(8,128)(2,1)S(1)}, u32[]{:S(2)}) copy-start(bf16[192,1024]{1,0:T(8,128)(2,1)S(1)} %get-tuple-element.68.rows_ref) | copy-start | bytes 1179652
  136.8 1.8 copy-start.11
  138.7 1.3 copy-start.13
  139.9 13.9 %copy-start.15 = (bf16[768,384]{1,0:T(8,128)(2,1)S(1)}, bf16[768,384]{1,0:T(8,128)(2,1)}, u32[]{:S(2)}) copy-start(bf16[768,384]{1,0:T(8,128)(2,1)} %copy-done.14) | copy-start | bytes 1769476
  176.1 52.2 %all-to-all-start.2 = ((bf16[64,24,1024]{2,1,0:T(8,128)(2,1)}), bf16[64,24,1024]{2,1,0:T(8,128)(2,1)S(1)}, u32[]{:S(2)}, u32[]{:S(2)}) async-start(bf16[64,24,1024]{2,1,0:T(8,128)(2,1)} %bitcast.24), calls=%async_computation.2 | async-start | bytes 6291456 | tf_op jit(solution)/shard_map/all_to_all | solution.py:388
  181.2 1.1 copy-start.5
  182.3 1.1 copy-start.7
  183.3 1.0 copy-start.9
  188.9 32.5 %collective-permute-start = (bf16[48,1152]{1,0:T(8,128)(2,1)S(1)}, bf16[48,1152]{1,0:T(8,128)(2,1)S(1)}, u32[]{:S(2)}, u32[]{:S(2)}) collective-permute-start(bf16[48,1152]{1,0:T(8,128)(2,1)S(1)} %get-tuple-element.73), channel_id=1, source_target_pairs={{0,8},{8,16},{16,24},{24,0},{1,9},{9,17},{17,25},{25,1},{2,10},{10... | collective-permute-start | bytes 331784 | tf_op jit(solution)/shard_map/ppermute | solution.py:363
  189.9 38.3 %collective-permute-start.1 = (bf16[48,1152]{1,0:T(8,128)(2,1)S(1)}, bf16[48,1152]{1,0:T(8,128)(2,1)S(1)}, u32[]{:S(2)}, u32[]{:S(2)}) collective-permute-start(bf16[48,1152]{1,0:T(8,128)(2,1)S(1)} %get-tuple-element.74), channel_id=1, source_target_pairs={{0,16},{8,24},{16,0},{24,8},{1,17},{9,25},{17,1},{25,9},{2,18},{10... | collective-permute-start | bytes 331784 | tf_op jit(solution)/shard_map/ppermute | solution.py:363
  192.0 36.3 %collective-permute-start.2 = (bf16[48,1152]{1,0:T(8,128)(2,1)S(1)}, bf16[48,1152]{1,0:T(8,128)(2,1)S(1)}, u32[]{:S(2)}, u32[]{:S(2)}) collective-permute-start(bf16[48,1152]{1,0:T(8,128)(2,1)S(1)} %get-tuple-element.75), channel_id=1, source_target_pairs={{0,24},{8,0},{16,8},{24,16},{1,25},{9,1},{17,9},{25,17},{2,26},{10... | collective-permute-start | bytes 331784 | tf_op jit(solution)/shard_map/ppermute | solution.py:363
  228.3 0.7 copy-start.16
  229.6 1.1 copy-start.1
  232.0 10.6 %collective-permute-start.3 = (bf16[48,1024]{1,0:T(8,128)(2,1)S(1)}, bf16[48,1024]{1,0:T(8,128)(2,1)S(1)}, u32[]{:S(2)}, u32[]{:S(2)}) collective-permute-start(bf16[48,1024]{1,0:T(8,128)(2,1)S(1)} %get-tuple-element.80), channel_id=1, source_target_pairs={{0,8},{8,16},{16,24},{24,0},{1,9},{9,17},{17,25},{25,1},{2,10},{10... | collective-permute-start | bytes 294920 | tf_op jit(solution)/shard_map/ppermute | solution.py:363
  232.1 10.5 %collective-permute-start.4 = (bf16[48,1024]{1,0:T(8,128)(2,1)S(1)}, bf16[48,1024]{1,0:T(8,128)(2,1)S(1)}, u32[]{:S(2)}, u32[]{:S(2)}) collective-permute-start(bf16[48,1024]{1,0:T(8,128)(2,1)S(1)} %get-tuple-element.81), channel_id=1, source_target_pairs={{0,16},{8,24},{16,0},{24,8},{1,17},{9,25},{17,1},{25,9},{2,18},{10... | collective-permute-start | bytes 294920 | tf_op jit(solution)/shard_map/ppermute | solution.py:363
  234.9 11.0 %collective-permute-start.5 = (bf16[48,1024]{1,0:T(8,128)(2,1)S(1)}, bf16[48,1024]{1,0:T(8,128)(2,1)S(1)}, u32[]{:S(2)}, u32[]{:S(2)}) collective-permute-start(bf16[48,1024]{1,0:T(8,128)(2,1)S(1)} %get-tuple-element.82), channel_id=1, source_target_pairs={{0,24},{8,0},{16,8},{24,16},{1,25},{9,1},{17,9},{25,17},{2,26},{10... | collective-permute-start | bytes 294920 | tf_op jit(solution)/shard_map/ppermute | solution.py:363
where the time goes:
time: 248 us; the launch traced here: 247 us
  blocking collectives  108 us (44%)
  waiting for transfers between devices  51.9 us (21%)
  Pallas kernels  47 us (19%)
  starting transfers between devices  23.6 us (10%)
  local copies, waits for them, and re-layouts  13.1 us (5%)
  other arithmetic  3.14 us (1%)
    all_to_all x1, blocking collectives, exchange(): lax.all_to_all(rows.reshape(dests, slots, columns), SPREAD, split_axis=0,...  85.7 us
    ppermute x6, waiting for transfers between devices, sum_blocks(): moved = lax.ppermute(rows, 'zhi', [(i, (i + step) % n) for i in range(n)])  39 us
    pallas_call x2, Pallas kernels, expert_call(): pl.pallas_call(functools.partial(kernel, slots), grid=(steps,), in_specs=...  24.8 us
    all_gather x1, blocking collectives, body(): rows = lax.all_gather(own, 'zhi', axis=0, tiled=True)  22.2 us
    all_to_all x2, waiting for transfers between devices, exchange(): lax.all_to_all(rows.reshape(dests, slots, columns), SPREAD, split_axis=0,...  13 us
    ppermute x6, starting transfers between devices, sum_blocks(): moved = lax.ppermute(rows, 'zhi', [(i, (i + step) % n) for i in range(n)])  12.9 us
    unnamed x35, local copies, waits for them, and re-layouts  12.3 us
    all_to_all x2, starting transfers between devices, exchange(): lax.all_to_all(rows.reshape(dests, slots, columns), SPREAD, split_axis=0,...  10.7 us
  transfers between devices with their start and end apart: 8, of which 5 were waited for; matrix products, arithmetic and copies ran while one was open for 1% of the time, Pallas kernels for 11%

commit v1 on v0

--- a/solution.py
+++ b/solution.py
@@ -12,7 +12,6 @@
 F32 = jnp.float32
 SPREAD = ("y", "core", "zlo", "x")
 EXTRA = 128
-SORT = 8
 STEPS = (0, 1, 2, 3)
 INNER = (((0,), (0,)), ((), ()))
 OUTER = (((1,), (1,)), ((), ()))
@@ -86,13 +85,26 @@
     )(tokens, out_grad, experts_t, gates_t)
 
 
-def fill_kernel(here, top, slots, rows_ref, expert_ref, out_ref, code_ref, weight_ref, ids_ref):
+def dest_experts(index, slot_map, dests):
+    groups, members = slot_map.shape
+    near = dests // groups
+    row = (iota((dests, groups), 0) // near == iota((dests, groups), 1)).astype(BF)
+    held = jnp.dot(row, slot_map.astype(F32).astype(BF), preferred_element_type=F32)
+    column = index * near + iota((dests, members), 0) % near
+    held = jnp.sum(jnp.where(iota((dests, members), 1) == column, held, 0.0), axis=1, keepdims=True)
+    first = iota((dests, 1), 0) // near * (members // 2)
+    return (held.astype(jnp.int32) // 2 + first).astype(F32)
+
+
+def fill_kernel(here, top, slots, index_ref, rows_ref, map_ref, out_ref, code_ref, weight_ref, ids_ref, expert_ref):
     held, width = rows_ref.shape[0], out_ref.shape[1]
     step = pl.program_id(0)
 
     @pl.when(step == 0)
     def _():
-        make_tables(here, top, slots, rows_ref[:, width:], expert_ref[...][:, :1], code_ref, weight_ref, ids_ref)
+        dest_expert = dest_experts(index_ref[0, 0], map_ref[...], code_ref.shape[0])
+        make_tables(here, top, slots, rows_ref[:, width:], dest_expert, code_ref, weight_ref, ids_ref)
+        expert_ref[...] = jnp.broadcast_to(dest_expert, expert_ref.shape)
 
     part = out_ref.shape[0] // slots
     at = pl.ds(pl.multiple_of(step * part, part), part)
@@ -105,15 +117,14 @@
     out_ref[...] = (scale * raw).astype(BF)
 
 
-def fill(rows, dest_expert, here, top, slots, width, steps=4):
+def fill(index, rows, slot_map, dests, here, top, slots, width, steps=4):
     held = rows.shape[0]
-    dests = dest_expert.shape[0]
     part = dests // steps * slots
-    tables = [(dests, held), (dests, held), (top, held)]
+    tables = [(dests, held), (dests, held), (top, held), (dests, 128)]
     return pl.pallas_call(
         functools.partial(fill_kernel, here, top, slots),
         grid=(steps,),
-        in_specs=[whole(rows), whole(dest_expert)],
+        in_specs=[pl.BlockSpec(memory_space=pltpu.SMEM), whole(rows), whole(slot_map)],
         out_specs=[pl.BlockSpec((part, width), lambda i: (i, 0))]
         + [pl.BlockSpec(shape, lambda i: (0, 0)) for shape in tables],
         out_shape=[jax.ShapeDtypeStruct((dests * slots, width), BF)]
@@ -121,61 +132,45 @@
         compiler_params=params(),
         cost_estimate=cost(2 * dests * slots * held * width, 2 * dests * slots * width),
         name="fill",
-    )(rows, dest_expert)
-
-
-def sorting(slots, transposed=False):
-    half, count = slots // 2, SORT * slots
-    a, b = iota((count, count), 0), iota((count, count), 1)
-    if transposed:
-        a, b = b, a
-    kind, place = a // (SORT * half), a % (SORT * half)
-    return (place // half * slots + kind * half + place % half == b).astype(BF)
-
-
-def sort_rows(order, rows):
-    return jnp.dot(order, rows, preferred_element_type=F32).astype(BF)
+    )(index, rows, slot_map)
 
 
 def kind_rows(kind, slots, rows_ref):
-    count = SORT * slots
-    half = count // 2
-    place, at = iota((half, count), 0), iota((half, count), 1)
-    order = (place // (slots // 2) * slots + kind * (slots // 2) + place % (slots // 2) == at).astype(BF)
-    parts = [sort_rows(order, rows_ref[i : i + count, :]) for i in range(0, rows_ref.shape[0], count)]
-    return jnp.concatenate(parts, axis=0)
+    half = slots // 2
+    starts = range(kind * half, rows_ref.shape[0], slots)
+    return jnp.concatenate([rows_ref[i : i + half, :] for i in starts], axis=0)
 
 
 def split_rows(slots, rows, out_ref):
-    order = sorting(slots, transposed=True)
-    count = order.shape[0]
-    half, features = count // 2, rows.shape[1] // 2
-    for i in range(rows.shape[0] // half):
-        part = rows[i * half : (i + 1) * half]
-        both = jnp.concatenate([part[:, :features], part[:, features:]], axis=0)
-        out_ref[i * count : (i + 1) * count, :] = sort_rows(order, both)
-
-
-def forward_kernel(slots, rows_ref, gate_ref, up_ref, down_ref, out_ref, hidden_ref, active_ref, slope_ref):
+    half, features = slots // 2, rows.shape[1] // 2
+    parts = []
+    for i in range(0, rows.shape[0], half):
+        parts += [rows[i : i + half, :features], rows[i : i + half, features:]]
+    out_ref[...] = jnp.concatenate(parts, axis=0)
+
+
+def forward_kernel(slots, rows_ref, gate_ref, up_ref, down_ref, out_ref):
     slot_rows = kind_rows(0, slots, rows_ref)
     gate_pre = jnp.dot(slot_rows, gate_ref[...], preferred_element_type=F32)
     up_pre = jnp.dot(slot_rows, up_ref[...], preferred_element_type=F32)
+    hidden = (gate_pre * jax.nn.sigmoid(gate_pre) * up_pre).astype(BF)
+    partial_rows = jnp.dot(hidden, down_ref[...], preferred_element_type=F32).astype(BF)
+    split_rows(slots, partial_rows, out_ref)
+
+
+def backward_kernel(slots, rows_ref, gate_ref, up_ref, down_ref, out_ref, hidden_ref, gate_grad_ref, up_grad_ref):
+    slot_rows = kind_rows(0, slots, rows_ref)
+    scaled = kind_rows(1, slots, rows_ref)
+    gate_pre = jnp.dot(slot_rows, gate_ref[...], preferred_element_type=F32)
+    up_pre = jnp.dot(slot_rows, up_ref[...], preferred_element_type=F32)
+    hidden_grad = lax.dot_general(scaled, down_ref[...], OUTER, preferred_element_type=F32)
     sigmoid_gate = jax.nn.sigmoid(gate_pre)
     active = gate_pre * sigmoid_gate
-    hidden = (active * up_pre).astype(BF)
-    hidden_ref[...] = hidden
-    active_ref[...] = active
-    slope_ref[...] = up_pre * sigmoid_gate * (1.0 + gate_pre * (1.0 - sigmoid_gate))
-    partial_rows = jnp.dot(hidden, down_ref[...], preferred_element_type=F32).astype(BF)
-    split_rows(slots, partial_rows, out_ref)
-
-
-def backward_kernel(slots, rows_ref, active_ref, slope_ref, gate_ref, up_ref, down_ref,
-                    out_ref, gate_grad_ref, up_grad_ref):
-    scaled = kind_rows(1, slots, rows_ref)
-    hidden_grad = lax.dot_general(scaled, down_ref[...], OUTER, preferred_element_type=F32)
-    gate_pre_grad = (hidden_grad * slope_ref[...]).astype(BF)
-    up_pre_grad = (hidden_grad * active_ref[...]).astype(BF)
+    gate_pre_grad = (
+        hidden_grad * up_pre * sigmoid_gate * (1.0 + gate_pre * (1.0 - sigmoid_gate))
+    ).astype(BF)
+    up_pre_grad = (hidden_grad * active).astype(BF)
+    hidden_ref[...] = (active * up_pre).astype(BF)
     gate_grad_ref[...] = gate_pre_grad
     up_grad_ref[...] = up_pre_grad
     back_rows = (
@@ -185,35 +180,28 @@
     split_rows(slots, back_rows, out_ref)
 
 
-def expert_call(kernel, rows, kept, slabs, outs, name, slots, steps=4):
+def expert_call(kernel, rows, slabs, kept, name, slots, steps=4):
     count, width = rows.shape
     units = slabs[0].shape[1]
     chunk = lambda size, columns: pl.BlockSpec((size // steps, columns), lambda i: (i, 0))
     return pl.pallas_call(
         functools.partial(kernel, slots),
         grid=(steps,),
-        in_specs=[chunk(count, width)] + [chunk(count // 2, units)] * len(kept) + [whole(a) for a in slabs],
-        out_specs=[chunk(count, width // 2)] + [chunk(count // 2, units)] * len(outs),
+        in_specs=[chunk(count, width)] + [whole(a) for a in slabs],
+        out_specs=[chunk(count, width // 2)] + [chunk(count // 2, units)] * kept,
         out_shape=[jax.ShapeDtypeStruct((count, width // 2), BF)]
-        + [jax.ShapeDtypeStruct((count // 2, units), kind) for kind in outs],
+        + [jax.ShapeDtypeStruct((count // 2, units), BF)] * kept,
         compiler_params=params(),
         cost_estimate=cost(3 * count * units * width, 3 * count * width + 6 * units * width, count * units),
         name=name,
-    )(rows, *kept, *slabs)
-
-
-def slab_grad_kernel(slots, rows_ref, hidden_ref, gate_grad_ref, up_grad_ref, gate_out, up_out, down_out, token_ref, grad_ref):
-    count = SORT * slots
-    half = count // 2
-    order = sorting(slots)
-    for i in range(rows_ref.shape[0] // count):
-        rows = sort_rows(order, rows_ref[i * count : (i + 1) * count, :])
-        token_ref[i * half : (i + 1) * half, :] = rows[:half]
-        grad_ref[i * half : (i + 1) * half, :] = rows[half:]
-    slot_rows = token_ref[...]
+    )(rows, *slabs)
+
+
+def slab_grad_kernel(slots, rows_ref, hidden_ref, gate_grad_ref, up_grad_ref, gate_out, up_out, down_out):
+    slot_rows, scaled = kind_rows(0, slots, rows_ref), kind_rows(1, slots, rows_ref)
     gate_out[...] = lax.dot_general(slot_rows, gate_grad_ref[...], INNER, preferred_element_type=F32).astype(BF)
     up_out[...] = lax.dot_general(slot_rows, up_grad_ref[...], INNER, preferred_element_type=F32).astype(BF)
-    down_out[...] = lax.dot_general(hidden_ref[...], grad_ref[...], INNER, preferred_element_type=F32).astype(BF)
+    down_out[...] = lax.dot_general(hidden_ref[...], scaled, INNER, preferred_element_type=F32).astype(BF)
 
 
 def slab_grads(rows, hidden, gate_pre_grad, up_pre_grad, slots, steps=4):
@@ -227,7 +215,6 @@
         out_specs=[pl.BlockSpec((part, units), lambda i: (i, 0))] * 2
         + [pl.BlockSpec((units, part), lambda i: (0, i))],
         out_shape=[jax.ShapeDtypeStruct((width, units), BF)] * 2 + [jax.ShapeDtypeStruct((units, width), BF)],
-        scratch_shapes=[pltpu.VMEM((count // 2, part), BF)] * 2,
         compiler_params=params(),
         cost_estimate=cost(3 * count * units * width, 2 * count * width + 6 * units * width),
         name="slab_grads",
@@ -379,10 +366,6 @@
     own = pack(tokens, out_grad, experts.T, gate_values.T)
     rows = lax.all_gather(own, "zhi", axis=0, tiled=True)
 
-    column = lax.dynamic_slice_in_dim(slot_map, lax.axis_index("zhi") * near, near, axis=1)
-    dest_expert = column // 2 + jnp.arange(groups, dtype=jnp.int32)[:, None] * per_group
-    dest_expert = jnp.broadcast_to(dest_expert.reshape(dests, 1).astype(F32), (dests, 128))
-
     def exchange(rows):
         columns = rows.shape[1]
         moved = lax.all_to_all(
@@ -393,15 +376,13 @@
     after = lax.optimization_barrier
     index = lax.axis_index("zhi").astype(jnp.int32).reshape(1, 1)
     slabs = (gate_weight[0], up_weight[0], down_weight[0])
-    sent, code, weight, ids = fill(rows, dest_expert, here, top, slots, width)
+    sent, code, weight, ids, dest_expert = fill(index, rows, slot_map, dests, here, top, slots, width)
     arrived = exchange(sent)
-    partial_out, hidden, active, slope = expert_call(
-        forward_kernel, arrived, (), slabs, (BF, F32, F32), "forward", slots
-    )
+    (partial_out,) = expert_call(forward_kernel, arrived, slabs, 0, "forward", slots)
     partial_out, arrived, rows = after((partial_out, arrived, rows))
     partial_back = exchange(partial_out)
-    back_rows, gate_pre_grad, up_pre_grad = expert_call(
-        backward_kernel, arrived, (active, slope), slabs, (BF, BF), "backward", slots
+    back_rows, hidden, gate_pre_grad, up_pre_grad = expert_call(
+        backward_kernel, arrived, slabs, 3, "backward", slots
     )
     grad_gate, grad_up, grad_down = slab_grads(arrived, hidden, gate_pre_grad, up_pre_grad, slots)
     high, low, mask, grads = prepare(rows, code, weight, here, slots)

time: 248 us -> 241 us (0.972)
  local copies, waits for them, and re-layouts: 13.1 us -> 8.58 us
  Pallas kernels: 47 us -> 43 us
  waiting for transfers between devices: 51.9 us -> 55.5 us
    unnamed x35 -> x29, local copies, waits for them, and re-layouts: 12.3 us -> 8.56 us
    all_to_all x2, waiting for transfers between devices: 13 us -> 15.7 us  [exchange(): lax.all_to_all(rows.reshape(dests, slots, columns), SPREAD, split_axis=0,...]
    pallas_call x2, Pallas kernels: 24.8 us -> 22.3 us  [expert_call(): pl.pallas_call(functools.partial(kernel, slots), grid=(steps,), in_specs=...]
where the time goes in v1:
time: 241 us
  blocking collectives  108 us (45%)
  waiting for transfers between devices  55.5 us (23%)
  Pallas kernels  43 us (18%)
  starting transfers between devices  23.4 us (10%)
  local copies, waits for them, and re-layouts  8.58 us (4%)
    all_to_all x1, blocking collectives, exchange(): lax.all_to_all(rows.reshape(dests, slots, columns), SPREAD, split_axis=0,...  85.7 us
    ppermute x6, waiting for transfers between devices, sum_blocks(): moved = lax.ppermute(rows, 'zhi', [(i, (i + step) % n) for i in range(n)])  39.8 us
    pallas_call x2, Pallas kernels, expert_call(): pl.pallas_call(functools.partial(kernel, slots), grid=(steps,), in_specs=...  22.3 us
    all_gather x1, blocking collectives, body(): rows = lax.all_gather(own, 'zhi', axis=0, tiled=True)  22.2 us
    all_to_all x2, waiting for transfers between devices, exchange(): lax.all_to_all(rows.reshape(dests, slots, columns), SPREAD, split_axis=0,...  15.7 us
    ppermute x6, starting transfers between devices, sum_blocks(): moved = lax.ppermute(rows, 'zhi', [(i, (i + step) % n) for i in range(n)])  12.7 us
    all_to_all x2, starting transfers between devices, exchange(): lax.all_to_all(rows.reshape(dests, slots, columns), SPREAD, split_axis=0,...  10.7 us
    unnamed x29, local copies, waits for them, and re-layouts  8.56 us
  transfers between devices with their start and end apart: 8, of which 5 were waited for; matrix products, arithmetic and copies ran while one was open for 1% of the time, Pallas kernels for 11%

profile of v1, /device:TPU:1, one launch (start us, length us, event | category | flops | bytes accessed | tf_op | source)
XLA Modules:
  0.0 240.7 jit_solution(7237811286889855392)
XLA Ops:
  0.6 1.8 pack.1
  2.5 22.2 %all_gather.3.rows_ref = bf16[192,2176]{1,0:T(8,128)(2,1)S(1)} all-gather(bf16[48,2176]{1,0:T(8,128)(2,1)} %pack.1), channel_id=1, replica_groups=mesh['y'=4,'core'=2,'zhi'=4,'zlo'=2,'x'=4] {'zhi'}, dimensions={0}, use_global_device_ids=true | all-gather | bytes 1044480 | tf_op jit(solution)/shard_map/all_gather | solution.py:367
  24.7 0.0 copy-start.12
  24.7 0.7 copy-done.12
  25.4 4.6 %fill.1 = (bf16[1536,2048]{1,0:T(8,128)(2,1)}, f32[64,192]{1,0:T(8,128)S(1)}, f32[64,192]{1,0:T(8,128)S(1)}, f32[8,192]{1,0:T(8,128)S(1)}, f32[64,128]{1,0:T(8,128)S(1)}) custom-call(s32[1,1]{1,0:T(1,128)} %bitcast.index_ref, bf16[192,2176]{1,0:T(8,128)(2,1)S(1)} %all_gather.3.rows_ref, s32[8,32]{1,0:T(8,128)S(1)} %copy-done.12), custom_call_target="tpu_custom_call" | custom-call | flops 1207959552 | bytes 6291456 | tf_op jit(solution)/shard_map/fill/pallas_call | solution.py:124
  30.0 0.0 copy-start
  30.0 85.7 %all_to_all.15 = bf16[64,24,2048]{2,1,0:T(8,128)(2,1)} all-to-all(bf16[64,24,2048]{2,1,0:T(8,128)(2,1)} %bitcast.26), channel_id=1, replica_groups=mesh['y'=4,'core'=2,'zhi'=4,'zlo'=2,'x'=4] {'y','core','zlo','x'}, dimensions={0} | all-to-all | bytes 12582912 | tf_op jit(solution)/shard_map/all_to_all | solution.py:371
  115.7 0.0 copy-done
  115.7 0.0 copy-done.1
  115.7 0.0 copy-done.3
  115.7 8.7 %forward.1 = bf16[1536,1024]{1,0:T(8,128)(2,1)} custom-call(bf16[1536,2048]{1,0:T(8,128)(2,1)} %bitcast.22, bf16[2048,384]{1,0:T(8,128)(2,1)S(1)} %bitcast.16, bf16[2048,384]{1,0:T(8,128)(2,1)S(1)} %bitcast.18, bf16[384,2048]{1,0:T(8,128)(2,1)S(1)} %bitcast.21), custom_call_target="tpu_custom_call" | custom-call | flops 3623878656 | bytes 14155776 | tf_op jit(solution)/shard_map/forward/pallas_call | solution.py:187
  124.4 5.6 %all-to-all-start.1 = ((bf16[64,24,1024]{2,1,0:T(8,128)(2,1)}), bf16[64,24,1024]{2,1,0:T(8,128)(2,1)}, u32[]{:S(2)}, u32[]{:S(2)}) async-start(bf16[64,24,1024]{2,1,0:T(8,128)(2,1)} %bitcast.25), calls=%async_computation.1 | async-start | bytes 6291456 | tf_op jit(solution)/shard_map/all_to_all | solution.py:371
  130.1 0.7 prepare.1
  130.7 0.0 copy-start.8
  130.7 0.8 copy-done.8
  131.6 0.8 copy-done.10
  132.3 1.4 copy-done.2
  133.7 13.6 %backward.1 = (bf16[1536,1024]{1,0:T(8,128)(2,1)}, bf16[768,384]{1,0:T(8,128)(2,1)S(1)}, bf16[768,384]{1,0:T(8,128)(2,1)S(1)}, bf16[768,384]{1,0:T(8,128)(2,1)S(1)}) custom-call(bf16[1536,2048]{1,0:T(8,128)(2,1)} %bitcast.23, bf16[2048,384]{1,0:T(8,128)(2,1)S(1)} %bitcast.17, bf16[2048,384]{1,0:T(8,128)(2,1)S(1)} %bitcast.19, bf16[384,2048]{1,0:T(8,128)(2,1)} %bitcast.20), custom_call_target="tpu_custom_call" | custom-call | flops 3623878656 | bytes 14155776 | tf_op jit(solution)/shard_map/backward/pallas_call | solution.py:187
  147.4 0.0 copy-done.4
  147.4 0.0 copy-done.6
  147.4 7.8 %slab_grads.1 = (bf16[2048,384]{1,0:T(8,128)(2,1)}, bf16[2048,384]{1,0:T(8,128)(2,1)}, bf16[384,2048]{1,0:T(8,128)(2,1)}) custom-call(bf16[1536,2048]{1,0:T(8,128)(2,1)} %bitcast.24, bf16[768,384]{1,0:T(8,128)(2,1)S(1)} %get-tuple-element.55.hidden_ref, bf16[768,384]{1,0:T(8,128)(2,1)S(1)} %get-tuple-element.56.gate_grad_ref, ...), custom_call_target="tpu_custom_call" | custom-call | flops 3623878656 | bytes 11010048 | tf_op jit(solution)/shard_map/slab_grads/pallas_call | solution.py:211
  155.1 15.7 %all-to-all-done.1 = bf16[64,24,1024]{2,1,0:T(8,128)(2,1)} async-done(((bf16[64,24,1024]{2,1,0:T(8,128)(2,1)}), bf16[64,24,1024]{2,1,0:T(8,128)(2,1)}, u32[]{:S(2)}, u32[]{:S(2)}) %all-to-all-start.1) | async-done | bytes 3145760 | tf_op jit(solution)/shard_map/all_to_all | solution.py:371
  170.8 5.1 %all-to-all-start.2 = ((bf16[64,24,1024]{2,1,0:T(8,128)(2,1)}), bf16[64,24,1024]{2,1,0:T(8,128)(2,1)S(1)}, u32[]{:S(2)}, u32[]{:S(2)}) async-start(bf16[64,24,1024]{2,1,0:T(8,128)(2,1)} %bitcast.27), calls=%async_computation.2 | async-start | bytes 6291456 | tf_op jit(solution)/shard_map/all_to_all | solution.py:371
  175.9 0.0 copy-start.7
  175.9 1.1 copy-done.7
  177.0 1.1 copy-done.9
  178.1 1.0 copy-done.11
  179.1 4.6 %layer_sums.1 = (bf16[48,1152]{1,0:T(8,128)(2,1)S(1)}, bf16[48,1152]{1,0:T(8,128)(2,1)S(1)}, bf16[48,1152]{1,0:T(8,128)(2,1)S(1)}, bf16[48,1152]{1,0:T(8,128)(2,1)S(1)}) custom-call(s32[1,1]{1,0:T(1,128)} %bitcast.index_ref, bf16[1536,1024]{1,0:T(8,128)(2,1)} %bitcast.9.back_ref, bf16[192,1024]{1,0:T(8,128)(2,1)S(1)} %copy-done.11, ...), custom_call_target="tpu_custom_call" | custom-call | flops 1811939328 | bytes 3145728 | tf_op jit(solution)/shard_map/layer_sums/pallas_call | solution.py:303
  183.7 0.8 collective-permute-start
  184.5 2.2 collective-permute-start.1
  186.7 3.3 %collective-permute-start.2 = (bf16[48,1152]{1,0:T(8,128)(2,1)S(1)}, bf16[48,1152]{1,0:T(8,128)(2,1)S(1)}, u32[]{:S(2)}, u32[]{:S(2)}) collective-permute-start(bf16[48,1152]{1,0:T(8,128)(2,1)S(1)} %get-tuple-element.71), channel_id=1, source_target_pairs={{0,24},{8,0},{16,8},{24,16},{1,25},{9,1},{17,9},{25,17},{2,26},{10... | collective-permute-start | bytes 331784 | tf_op jit(solution)/shard_map/ppermute | solution.py:350
  190.0 26.2 %collective-permute-done = bf16[48,1152]{1,0:T(8,128)(2,1)S(1)} collective-permute-done((bf16[48,1152]{1,0:T(8,128)(2,1)S(1)}, bf16[48,1152]{1,0:T(8,128)(2,1)S(1)}, u32[]{:S(2)}, u32[]{:S(2)}) %collective-permute-start) | collective-permute-done | bytes 110624 | tf_op jit(solution)/shard_map/ppermute | solution.py:350
  216.2 6.8 %collective-permute-done.1 = bf16[48,1152]{1,0:T(8,128)(2,1)S(1)} collective-permute-done((bf16[48,1152]{1,0:T(8,128)(2,1)S(1)}, bf16[48,1152]{1,0:T(8,128)(2,1)S(1)}, u32[]{:S(2)}, u32[]{:S(2)}) %collective-permute-start.1) | collective-permute-done | bytes 110624 | tf_op jit(solution)/shard_map/ppermute | solution.py:350
  223.0 0.0 collective-permute-done.2
  223.0 0.7 convert_add_fusion
  223.7 0.0 all-to-all-done.2
  223.7 1.1 copy-done.5
  224.8 1.3 token_sums.1
  226.1 0.1 collective-permute-start.3
  226.2 2.8 %collective-permute-start.4 = (bf16[48,1024]{1,0:T(8,128)(2,1)S(1)}, bf16[48,1024]{1,0:T(8,128)(2,1)S(1)}, u32[]{:S(2)}, u32[]{:S(2)}) collective-permute-start(bf16[48,1024]{1,0:T(8,128)(2,1)S(1)} %get-tuple-element.77), channel_id=1, source_target_pairs={{0,16},{8,24},{16,0},{24,8},{1,17},{9,25},{17,1},{25,9},{2,18},{10... | collective-permute-start | bytes 294920 | tf_op jit(solution)/shard_map/ppermute | solution.py:350
  228.9 3.5 %collective-permute-start.5 = (bf16[48,1024]{1,0:T(8,128)(2,1)S(1)}, bf16[48,1024]{1,0:T(8,128)(2,1)S(1)}, u32[]{:S(2)}, u32[]{:S(2)}) collective-permute-start(bf16[48,1024]{1,0:T(8,128)(2,1)S(1)} %get-tuple-element.78), channel_id=1, source_target_pairs={{0,24},{8,0},{16,8},{24,16},{1,25},{9,1},{17,9},{25,17},{2,26},{10... | collective-permute-start | bytes 294920 | tf_op jit(solution)/shard_map/ppermute | solution.py:350
  232.4 0.0 copy-done.13
  232.5 0.7 copy.14
  233.1 3.7 %collective-permute-done.3 = bf16[48,1024]{1,0:T(8,128)(2,1)S(1)} collective-permute-done((bf16[48,1024]{1,0:T(8,128)(2,1)S(1)}, bf16[48,1024]{1,0:T(8,128)(2,1)S(1)}, u32[]{:S(2)}, u32[]{:S(2)}) %collective-permute-start.3) | collective-permute-done | bytes 98336 | tf_op jit(solution)/shard_map/ppermute | solution.py:350
  236.8 0.0 collective-permute-done.4
  236.8 3.1 %collective-permute-done.5 = bf16[48,1024]{1,0:T(8,128)(2,1)S(1)} collective-permute-done((bf16[48,1024]{1,0:T(8,128)(2,1)S(1)}, bf16[48,1024]{1,0:T(8,128)(2,1)S(1)}, u32[]{:S(2)}, u32[]{:S(2)}) %collective-permute-start.5) | collective-permute-done | bytes 98336 | tf_op jit(solution)/shard_map/ppermute | solution.py:350
  240.0 0.1 add_convert_fusion
  240.0 0.7 pad_maximum_fusion
  (14 shorter events, 0.1 us)
Async XLA Ops:
  24.7 0.7 copy-start.12
  30.0 85.7 %copy-start = (bf16[1,2048,384]{2,1,0:T(8,128)(2,1)S(1)}, bf16[1,2048,384]{2,1,0:T(8,128)(2,1)}, u32[]{:S(2)}) copy-start(bf16[1,2048,384]{2,1,0:T(8,128)(2,1)} %param.13) | copy-start | bytes 4718596
  30.0 85.7 %copy-start.1 = (bf16[1,2048,384]{2,1,0:T(8,128)(2,1)S(1)}, bf16[1,2048,384]{2,1,0:T(8,128)(2,1)}, u32[]{:S(2)}) copy-start(bf16[1,2048,384]{2,1,0:T(8,128)(2,1)} %param.14) | copy-start | bytes 4718596
  30.0 85.7 %copy-start.3 = (bf16[1,384,2048]{2,1,0:T(8,128)(2,1)S(1)}, bf16[1,384,2048]{2,1,0:T(8,128)(2,1)}, u32[]{:S(2)}) copy-start(bf16[1,384,2048]{2,1,0:T(8,128)(2,1)} %param.15) | copy-start | bytes 4718596
  124.4 46.4 %all-to-all-start.1 = ((bf16[64,24,1024]{2,1,0:T(8,128)(2,1)}), bf16[64,24,1024]{2,1,0:T(8,128)(2,1)}, u32[]{:S(2)}, u32[]{:S(2)}) async-start(bf16[64,24,1024]{2,1,0:T(8,128)(2,1)} %bitcast.25), calls=%async_computation.1 | async-start | bytes 6291456 | tf_op jit(solution)/shard_map/all_to_all | solution.py:371
  130.7 0.8 copy-start.8
  131.6 0.8 copy-start.10
  132.3 1.4 copy-start.2
  133.7 13.6 %copy-start.4 = (bf16[192,1536]{1,0:T(8,128)(2,1)}, bf16[192,1536]{1,0:T(8,128)(2,1)S(1)}, u32[]{:S(2)}) copy-start(bf16[192,1536]{1,0:T(8,128)(2,1)S(1)} %get-tuple-element.74.mask_ref) | copy-start | bytes 1769476
  133.7 13.6 %copy-start.6 = (bf16[192,1536]{1,0:T(8,128)(2,1)}, bf16[192,1536]{1,0:T(8,128)(2,1)S(1)}, u32[]{:S(2)}) copy-start(bf16[192,1536]{1,0:T(8,128)(2,1)S(1)} %get-tuple-element.66.high_ref) | copy-start | bytes 1769476
  170.8 52.9 %all-to-all-start.2 = ((bf16[64,24,1024]{2,1,0:T(8,128)(2,1)}), bf16[64,24,1024]{2,1,0:T(8,128)(2,1)S(1)}, u32[]{:S(2)}, u32[]{:S(2)}) async-start(bf16[64,24,1024]{2,1,0:T(8,128)(2,1)} %bitcast.27), calls=%async_computation.2 | async-start | bytes 6291456 | tf_op jit(solution)/shard_map/all_to_all | solution.py:371
  175.9 1.1 copy-start.7
  177.0 1.1 copy-start.9
  178.1 1.0 copy-start.11
  183.7 32.5 %collective-permute-start = (bf16[48,1152]{1,0:T(8,128)(2,1)S(1)}, bf16[48,1152]{1,0:T(8,128)(2,1)S(1)}, u32[]{:S(2)}, u32[]{:S(2)}) collective-permute-start(bf16[48,1152]{1,0:T(8,128)(2,1)S(1)} %get-tuple-element.69), channel_id=1, source_target_pairs={{0,8},{8,16},{16,24},{24,0},{1,9},{9,17},{17,25},{25,1},{2,10},{10... | collective-permute-start | bytes 331784 | tf_op jit(solution)/shard_map/ppermute | solution.py:350
  184.5 38.5 %collective-permute-start.1 = (bf16[48,1152]{1,0:T(8,128)(2,1)S(1)}, bf16[48,1152]{1,0:T(8,128)(2,1)S(1)}, u32[]{:S(2)}, u32[]{:S(2)}) collective-permute-start(bf16[48,1152]{1,0:T(8,128)(2,1)S(1)} %get-tuple-element.70), channel_id=1, source_target_pairs={{0,16},{8,24},{16,0},{24,8},{1,17},{9,25},{17,1},{25,9},{2,18},{10... | collective-permute-start | bytes 331784 | tf_op jit(solution)/shard_map/ppermute | solution.py:350
  186.7 36.3 %collective-permute-start.2 = (bf16[48,1152]{1,0:T(8,128)(2,1)S(1)}, bf16[48,1152]{1,0:T(8,128)(2,1)S(1)}, u32[]{:S(2)}, u32[]{:S(2)}) collective-permute-start(bf16[48,1152]{1,0:T(8,128)(2,1)S(1)} %get-tuple-element.71), channel_id=1, source_target_pairs={{0,24},{8,0},{16,8},{24,16},{1,25},{9,1},{17,9},{25,17},{2,26},{10... | collective-permute-start | bytes 331784 | tf_op jit(solution)/shard_map/ppermute | solution.py:350
  223.7 1.1 copy-start.5
  224.8 7.7 %copy-start.13 = (f32[48,1152]{1,0:T(8,128)S(1)}, f32[48,1152]{1,0:T(8,128)}, u32[]{:S(2)}) copy-start(f32[48,1152]{1,0:T(8,128)} %convert_add_fusion) | copy-start | bytes 663556
  226.1 10.8 %collective-permute-start.3 = (bf16[48,1024]{1,0:T(8,128)(2,1)S(1)}, bf16[48,1024]{1,0:T(8,128)(2,1)S(1)}, u32[]{:S(2)}, u32[]{:S(2)}) collective-permute-start(bf16[48,1024]{1,0:T(8,128)(2,1)S(1)} %get-tuple-element.76), channel_id=1, source_target_pairs={{0,8},{8,16},{16,24},{24,0},{1,9},{9,17},{17,25},{25,1},{2,10},{10... | collective-permute-start | bytes 294920 | tf_op jit(solution)/shard_map/ppermute | solution.py:350
  226.2 10.7 %collective-permute-start.4 = (bf16[48,1024]{1,0:T(8,128)(2,1)S(1)}, bf16[48,1024]{1,0:T(8,128)(2,1)S(1)}, u32[]{:S(2)}, u32[]{:S(2)}) collective-permute-start(bf16[48,1024]{1,0:T(8,128)(2,1)S(1)} %get-tuple-element.77), channel_id=1, source_target_pairs={{0,16},{8,24},{16,0},{24,8},{1,17},{9,25},{17,1},{25,9},{2,18},{10... | collective-permute-start | bytes 294920 | tf_op jit(solution)/shard_map/ppermute | solution.py:350
  228.9 11.0 %collective-permute-start.5 = (bf16[48,1024]{1,0:T(8,128)(2,1)S(1)}, bf16[48,1024]{1,0:T(8,128)(2,1)S(1)}, u32[]{:S(2)}, u32[]{:S(2)}) collective-permute-start(bf16[48,1024]{1,0:T(8,128)(2,1)S(1)} %get-tuple-element.78), channel_id=1, source_target_pairs={{0,24},{8,0},{16,8},{24,16},{1,25},{9,1},{17,9},{25,17},{2,26},{10... | collective-permute-start | bytes 294920 | tf_op jit(solution)/shard_map/ppermute | solution.py:350

commit v2 on v1

--- a/solution.py
+++ b/solution.py
@@ -10,7 +10,7 @@
 
 BF = jnp.bfloat16
 F32 = jnp.float32
-SPREAD = ("y", "core", "zlo", "x")
+SPREAD = ("zlo", "x", "y", "core")
 EXTRA = 128
 STEPS = (0, 1, 2, 3)
 INNER = (((0,), (0,)), ((), ()))
@@ -34,8 +34,8 @@
     return pl.CostEstimate(flops=flops, bytes_accessed=moved, transcendentals=special)
 
 
-def params():
-    return pltpu.CompilerParams(vmem_limit_bytes=VMEM_LIMIT)
+def params(limit=VMEM_LIMIT):
+    return pltpu.CompilerParams(vmem_limit_bytes=limit)
 
 
 def make_tables(here, top, slots, info, dest_expert, code_ref, weight_ref, ids_ref):
@@ -60,7 +60,18 @@
     ids_ref[...] = ids
 
 
-def pack_kernel(tokens_ref, out_grad_ref, experts_ref, gates_ref, out_ref):
+def dest_experts(index, slot_map, dests):
+    groups, members = slot_map.shape
+    near = dests // groups
+    row = (iota((dests, groups), 0) % groups == iota((dests, groups), 1)).astype(BF)
+    held = jnp.dot(row, slot_map.astype(F32).astype(BF), preferred_element_type=F32)
+    column = index * near + iota((dests, members), 0) // groups
+    held = jnp.sum(jnp.where(iota((dests, members), 1) == column, held, 0.0), axis=1, keepdims=True)
+    first = iota((dests, 1), 0) % groups * (members // 2)
+    return (held.astype(jnp.int32) // 2 + first).astype(F32)
+
+
+def pack_kernel(index_ref, tokens_ref, out_grad_ref, experts_ref, gates_ref, map_ref, out_ref, expert_ref):
     here, width = tokens_ref.shape
     top = experts_ref.shape[0]
     gates = gates_ref[...]
@@ -71,40 +82,33 @@
     for k, part in enumerate((experts_ref[...].astype(F32).astype(BF), high, middle, low)):
         place = (iota((top, EXTRA), 0) + k * top == iota((top, EXTRA), 1)).astype(BF)
         extra += lax.dot_general(part, place, INNER, preferred_element_type=F32)
+    held = dest_experts(index_ref[0, 0], map_ref[...], expert_ref.shape[0])
+    expert_ref[...] = jnp.broadcast_to(held, expert_ref.shape)
     rows = [tokens_ref[...].astype(F32), out_grad_ref[...].astype(F32)]
     out_ref[:, :width] = jnp.concatenate(rows, axis=0).astype(BF)
     out_ref[:, width:] = jnp.concatenate([extra, extra], axis=0).astype(BF)
 
 
-def pack(tokens, out_grad, experts_t, gates_t):
+def pack(index, tokens, out_grad, experts_t, gates_t, slot_map, dests):
     here, width = tokens.shape
     return pl.pallas_call(
         pack_kernel,
-        out_shape=jax.ShapeDtypeStruct((2 * here, width + EXTRA), BF),
+        in_specs=[pl.BlockSpec(memory_space=pltpu.SMEM)] + [pl.BlockSpec(memory_space=pltpu.VMEM)] * 5,
+        out_shape=[
+            jax.ShapeDtypeStruct((2 * here, width + EXTRA), BF),
+            jax.ShapeDtypeStruct((dests, 128), F32),
+        ],
         name="pack",
-    )(tokens, out_grad, experts_t, gates_t)
-
-
-def dest_experts(index, slot_map, dests):
-    groups, members = slot_map.shape
-    near = dests // groups
-    row = (iota((dests, groups), 0) // near == iota((dests, groups), 1)).astype(BF)
-    held = jnp.dot(row, slot_map.astype(F32).astype(BF), preferred_element_type=F32)
-    column = index * near + iota((dests, members), 0) % near
-    held = jnp.sum(jnp.where(iota((dests, members), 1) == column, held, 0.0), axis=1, keepdims=True)
-    first = iota((dests, 1), 0) // near * (members // 2)
-    return (held.astype(jnp.int32) // 2 + first).astype(F32)
-
-
-def fill_kernel(here, top, slots, index_ref, rows_ref, map_ref, out_ref, code_ref, weight_ref, ids_ref, expert_ref):
+    )(index, tokens, out_grad, experts_t, gates_t, slot_map)
+
+
+def fill_kernel(here, top, slots, rows_ref, expert_ref, out_ref, code_ref, weight_ref, ids_ref):
     held, width = rows_ref.shape[0], out_ref.shape[1]
     step = pl.program_id(0)
 
     @pl.when(step == 0)
     def _():
-        dest_expert = dest_experts(index_ref[0, 0], map_ref[...], code_ref.shape[0])
-        make_tables(here, top, slots, rows_ref[:, width:], dest_expert, code_ref, weight_ref, ids_ref)
-        expert_ref[...] = jnp.broadcast_to(dest_expert, expert_ref.shape)
+        make_tables(here, top, slots, rows_ref[:, width:], expert_ref[...][:, :1], code_ref, weight_ref, ids_ref)
 
     part = out_ref.shape[0] // slots
     at = pl.ds(pl.multiple_of(step * part, part), part)
@@ -117,14 +121,15 @@
     out_ref[...] = (scale * raw).astype(BF)
 
 
-def fill(index, rows, slot_map, dests, here, top, slots, width, steps=4):
+def fill(rows, dest_expert, here, top, slots, width, steps=2):
     held = rows.shape[0]
+    dests = dest_expert.shape[0]
     part = dests // steps * slots
-    tables = [(dests, held), (dests, held), (top, held), (dests, 128)]
+    tables = [(dests, held), (dests, held), (top, held)]
     return pl.pallas_call(
         functools.partial(fill_kernel, here, top, slots),
         grid=(steps,),
-        in_specs=[pl.BlockSpec(memory_space=pltpu.SMEM), whole(rows), whole(slot_map)],
+        in_specs=[whole(rows), whole(dest_expert)],
         out_specs=[pl.BlockSpec((part, width), lambda i: (i, 0))]
         + [pl.BlockSpec(shape, lambda i: (0, 0)) for shape in tables],
         out_shape=[jax.ShapeDtypeStruct((dests * slots, width), BF)]
@@ -132,7 +137,7 @@
         compiler_params=params(),
         cost_estimate=cost(2 * dests * slots * held * width, 2 * dests * slots * width),
         name="fill",
-    )(index, rows, slot_map)
+    )(rows, dest_expert)
 
 
 def kind_rows(kind, slots, rows_ref):
@@ -312,7 +317,7 @@
             pltpu.VMEM((held, EXTRA), F32),
             pltpu.VMEM((count, held), F32),
         ],
-        compiler_params=params(),
+        compiler_params=params(20 * 1024 * 1024),
         cost_estimate=cost(6 * count * held * half, 2 * count * half),
         name="layer_sums",
     )(index, returned, rows, code, ids, dest_expert, high, low)
@@ -324,7 +329,7 @@
     store_blocks(index_ref, total_ref, outs, slice(None))
 
 
-def token_sums(index, returned, mask, steps=2):
+def token_sums(index, returned, mask, steps=1):
     count, half = returned.shape
     held = mask.shape[0]
     size = held // len(STEPS)
@@ -337,18 +342,24 @@
         out_specs=[chunk(size)] * len(STEPS),
         out_shape=[jax.ShapeDtypeStruct((size, half), BF)] * len(STEPS),
         scratch_shapes=[pltpu.VMEM((held, part), F32)],
-        compiler_params=params(),
+        compiler_params=params(20 * 1024 * 1024),
         cost_estimate=cost(2 * count * held * half, 2 * count * half),
         name="token_sums",
     )(index, returned, mask)
 
 
-def sum_blocks(sums):
+def send_blocks(parts):
     n = lax.axis_size("zhi")
-    total = sums[0].astype(F32)
-    for rows, step in zip(sums[1:], STEPS[1:]):
-        moved = lax.ppermute(rows, "zhi", [(i, (i + step) % n) for i in range(n)])
-        total += moved.astype(F32)
+    return [
+        lax.ppermute(rows, "zhi", [(i, (i + step) % n) for i in range(n)])
+        for rows, step in zip(parts, STEPS[1:])
+    ]
+
+
+def add_blocks(own, rest):
+    total = own.astype(F32)
+    for rows in rest:
+        total += rows.astype(F32)
     return total
 
 
@@ -363,7 +374,8 @@
     dests = groups * near
     slots = 2 * blocks * capacity
 
-    own = pack(tokens, out_grad, experts.T, gate_values.T)
+    index = lax.axis_index("zhi").astype(jnp.int32).reshape(1, 1)
+    own, dest_expert = pack(index, tokens, out_grad, experts.T, gate_values.T, slot_map, dests)
     rows = lax.all_gather(own, "zhi", axis=0, tiled=True)
 
     def exchange(rows):
@@ -374,9 +386,8 @@
         return moved.reshape(dests * slots, columns)
 
     after = lax.optimization_barrier
-    index = lax.axis_index("zhi").astype(jnp.int32).reshape(1, 1)
     slabs = (gate_weight[0], up_weight[0], down_weight[0])
-    sent, code, weight, ids, dest_expert = fill(index, rows, slot_map, dests, here, top, slots, width)
+    sent, code, weight, ids = fill(rows, dest_expert, here, top, slots, width)
     arrived = exchange(sent)
     (partial_out,) = expert_call(forward_kernel, arrived, slabs, 0, "forward", slots)
     partial_out, arrived, rows = after((partial_out, arrived, rows))
@@ -390,9 +401,13 @@
         (back_rows, partial_back, high, low, mask, grads, grad_gate, grad_up, grad_down)
     )
     back_back = exchange(back_rows)
-    layer = sum_blocks(layer_sums(index, partial_back, grads, code, ids, dest_expert, high, low, slots))
-    back_back, layer = after((back_back, layer))
-    token = sum_blocks(token_sums(index, back_back, mask))
+    own_layer, *layer_parts = layer_sums(index, partial_back, grads, code, ids, dest_expert, high, low, slots)
+    layer_rest = send_blocks(layer_parts)
+    back_back, own_layer = after((back_back, own_layer))
+    own_token, *token_parts = token_sums(index, back_back, mask)
+    token_rest = send_blocks(token_parts)
+    layer = add_blocks(own_layer, layer_rest)
+    token = add_blocks(own_token, token_rest)
 
     half = width // 2
     layer_out = jnp.concatenate([layer[:here, :half], layer[here:, :half]], axis=1).astype(BF)

time: 241 us -> 244 us (1.012)
  starting transfers between devices: 23.4 us -> 31.4 us
  waiting for transfers between devices: 55.5 us -> 48.3 us
    ppermute x6, waiting for transfers between devices: 39.8 us -> 7.24 us  [send_blocks(): lax.ppermute(rows, 'zhi', [(i, (i + step) % n) for i in range(n)])]
    all_to_all x2, waiting for transfers between devices: 15.7 us -> 41.1 us  [exchange(): lax.all_to_all(rows.reshape(dests, slots, columns), SPREAD, split_axis=0,...]
    all_to_all x2, starting transfers between devices: 10.7 us -> 19 us  [exchange(): lax.all_to_all(rows.reshape(dests, slots, columns), SPREAD, split_axis=0,...]
  transfers between devices with their start and end apart: 8 -> 8, of which waited for: 5 -> 4; matrix products, arithmetic and copies ran while one was open for 1% -> 1% of each run, Pallas kernels for 11% -> 12%
where the time goes in v2:
time: 244 us; the launch traced here: 241 us
  blocking collectives  107 us (44%)
  waiting for transfers between devices  48.3 us (20%)
  Pallas kernels  43.2 us (18%)
  starting transfers between devices  31.4 us (13%)
  local copies, waits for them, and re-layouts  8.63 us (4%)
    all_to_all x1, blocking collectives, exchange(): lax.all_to_all(rows.reshape(dests, slots, columns), SPREAD, split_axis=0,...  85.1 us
    all_to_all x2, waiting for transfers between devices, exchange(): lax.all_to_all(rows.reshape(dests, slots, columns), SPREAD, split_axis=0,...  41.1 us
    all_gather x1, blocking collectives, body(): rows = lax.all_gather(own, 'zhi', axis=0, tiled=True)  22.2 us
    pallas_call x2, Pallas kernels, expert_call(): pl.pallas_call(functools.partial(kernel, slots), grid=(steps,), in_specs=...  22.1 us
    all_to_all x2, starting transfers between devices, exchange(): lax.all_to_all(rows.reshape(dests, slots, columns), SPREAD, split_axis=0,...  19 us
    ppermute x6, starting transfers between devices, send_blocks(): lax.ppermute(rows, 'zhi', [(i, (i + step) % n) for i in range(n)])  12.4 us
    unnamed x29, local copies, waits for them, and re-layouts  8.61 us
    pallas_call x1, Pallas kernels, slab_grads(): pl.pallas_call(functools.partial(slab_grad_kernel, slots), grid=(steps,),...  7.74 us
  transfers between devices with their start and end apart: 8, of which 4 were waited for; matrix products, arithmetic and copies ran while one was open for 1% of the time, Pallas kernels for 12%

profile of v2, /device:TPU:1, one launch (start us, length us, event | category | flops | bytes accessed | tf_op | source)
XLA Modules:
  0.0 241.5 jit_solution(1772456484617356260)
XLA Ops:
  0.6 1.9 pack.1
  2.5 22.2 %all_gather.3.rows_ref = bf16[192,2176]{1,0:T(8,128)(2,1)S(1)} all-gather(bf16[48,2176]{1,0:T(8,128)(2,1)} %get-tuple-element.45), channel_id=1, replica_groups=mesh['y'=4,'core'=2,'zhi'=4,'zlo'=2,'x'=4] {'zhi'}, dimensions={0}, use_global_device_ids=true | all-gather | bytes 1044480 | tf_op jit(solution)/shard_map/all_gather | solution.py:379
  24.7 0.0 copy-start.12
  24.7 0.8 copy-done.12
  25.5 4.1 %fill.1 = (bf16[1536,2048]{1,0:T(8,128)(2,1)}, f32[64,192]{1,0:T(8,128)S(1)}, f32[64,192]{1,0:T(8,128)S(1)}, f32[8,192]{1,0:T(8,128)S(1)}) custom-call(bf16[192,2176]{1,0:T(8,128)(2,1)S(1)} %all_gather.3.rows_ref, f32[64,128]{1,0:T(8,128)S(1)} %copy-done.12), custom_call_target="tpu_custom_call" | custom-call | flops 1207959552 | bytes 6291456 | tf_op jit(solution)/shard_map/fill/pallas_call | solution.py:129
  29.6 0.0 copy-start
  29.6 85.1 %all_to_all.15 = bf16[64,24,2048]{2,1,0:T(8,128)(2,1)} all-to-all(bf16[64,24,2048]{2,1,0:T(8,128)(2,1)} %bitcast.26), channel_id=1, replica_groups=mesh['y'=4,'core'=2,'zhi'=4,'zlo'=2,'x'=4] {'zlo','x','y','core'}, dimensions={0} | all-to-all | bytes 12582912 | tf_op jit(solution)/shard_map/all_to_all | solution.py:383
  114.7 0.0 copy-done
  114.7 0.0 copy-done.1
  114.7 0.0 copy-done.3
  114.7 8.5 %forward.1 = bf16[1536,1024]{1,0:T(8,128)(2,1)} custom-call(bf16[1536,2048]{1,0:T(8,128)(2,1)} %bitcast.22, bf16[2048,384]{1,0:T(8,128)(2,1)S(1)} %bitcast.16, bf16[2048,384]{1,0:T(8,128)(2,1)S(1)} %bitcast.18, bf16[384,2048]{1,0:T(8,128)(2,1)S(1)} %bitcast.21), custom_call_target="tpu_custom_call" | custom-call | flops 3623878656 | bytes 14155776 | tf_op jit(solution)/shard_map/forward/pallas_call | solution.py:192
  123.2 11.0 %all-to-all-start.1 = ((bf16[64,24,1024]{2,1,0:T(8,128)(2,1)}), bf16[64,24,1024]{2,1,0:T(8,128)(2,1)}, u32[]{:S(2)}, u32[]{:S(2)}) async-start(bf16[64,24,1024]{2,1,0:T(8,128)(2,1)} %bitcast.25), calls=%async_computation.1 | async-start | bytes 6291456 | tf_op jit(solution)/shard_map/all_to_all | solution.py:383
  134.3 0.7 prepare.1
  134.9 0.0 copy-start.8
  134.9 0.8 copy-done.8
  135.8 0.8 copy-done.10
  136.5 1.4 copy-done.2
  137.9 13.6 %backward.1 = (bf16[1536,1024]{1,0:T(8,128)(2,1)}, bf16[768,384]{1,0:T(8,128)(2,1)S(1)}, bf16[768,384]{1,0:T(8,128)(2,1)S(1)}, bf16[768,384]{1,0:T(8,128)(2,1)S(1)}) custom-call(bf16[1536,2048]{1,0:T(8,128)(2,1)} %bitcast.23, bf16[2048,384]{1,0:T(8,128)(2,1)S(1)} %bitcast.17, bf16[2048,384]{1,0:T(8,128)(2,1)S(1)} %bitcast.19, bf16[384,2048]{1,0:T(8,128)(2,1)} %bitcast.20), custom_call_target="tpu_custom_call" | custom-call | flops 3623878656 | bytes 14155776 | tf_op jit(solution)/shard_map/backward/pallas_call | solution.py:192
  151.5 0.0 copy-done.4
  151.5 0.0 copy-done.6
  151.5 7.7 %slab_grads.1 = (bf16[2048,384]{1,0:T(8,128)(2,1)}, bf16[2048,384]{1,0:T(8,128)(2,1)}, bf16[384,2048]{1,0:T(8,128)(2,1)}) custom-call(bf16[1536,2048]{1,0:T(8,128)(2,1)} %bitcast.24, bf16[768,384]{1,0:T(8,128)(2,1)S(1)} %get-tuple-element.58.hidden_ref, bf16[768,384]{1,0:T(8,128)(2,1)S(1)} %get-tuple-element.59.gate_grad_ref, ...), custom_call_target="tpu_custom_call" | custom-call | flops 3623878656 | bytes 11010048 | tf_op jit(solution)/shard_map/slab_grads/pallas_call | solution.py:216
  159.3 14.8 %all-to-all-done.1 = bf16[64,24,1024]{2,1,0:T(8,128)(2,1)} async-done(((bf16[64,24,1024]{2,1,0:T(8,128)(2,1)}), bf16[64,24,1024]{2,1,0:T(8,128)(2,1)}, u32[]{:S(2)}, u32[]{:S(2)}) %all-to-all-start.1) | async-done | bytes 3145760 | tf_op jit(solution)/shard_map/all_to_all | solution.py:383
  174.1 7.9 %all-to-all-start.2 = ((bf16[64,24,1024]{2,1,0:T(8,128)(2,1)}), bf16[64,24,1024]{2,1,0:T(8,128)(2,1)S(1)}, u32[]{:S(2)}, u32[]{:S(2)}) async-start(bf16[64,24,1024]{2,1,0:T(8,128)(2,1)} %bitcast.27), calls=%async_computation.2 | async-start | bytes 6291456 | tf_op jit(solution)/shard_map/all_to_all | solution.py:383
  182.0 0.0 copy-done.13
  182.0 0.0 copy-start.7
  182.0 1.1 copy-done.7
  183.1 1.1 copy-done.9
  184.1 1.0 copy-done.11
  185.1 5.3 %layer_sums.1 = (bf16[48,1152]{1,0:T(8,128)(2,1)S(1)}, bf16[48,1152]{1,0:T(8,128)(2,1)}, bf16[48,1152]{1,0:T(8,128)(2,1)}, bf16[48,1152]{1,0:T(8,128)(2,1)S(1)}) custom-call(s32[1,1]{1,0:T(1,128)} %bitcast.index_ref, bf16[1536,1024]{1,0:T(8,128)(2,1)} %bitcast.9.back_ref, bf16[192,1024]{1,0:T(8,128)(2,1)S(1)} %copy-done.11, ...), custom_call_target="tpu_custom_call" | custom-call | flops 1811939328 | bytes 3145728 | tf_op jit(solution)/shard_map/layer_sums/pallas_call | solution.py:308
  190.4 0.7 collective-permute-start
  191.1 2.1 collective-permute-start.1
  193.2 3.4 %collective-permute-start.2 = (bf16[48,1152]{1,0:T(8,128)(2,1)S(1)}, bf16[48,1152]{1,0:T(8,128)(2,1)}, u32[]{:S(2)}, u32[]{:S(2)}) collective-permute-start(bf16[48,1152]{1,0:T(8,128)(2,1)S(1)} %get-tuple-element.74), channel_id=1, source_target_pairs={{0,24},{8,0},{16,8},{24,16},{1,25},{9,1},{17,9},{25,17},{2,26},{10... | collective-permute-start | bytes 331784 | tf_op jit(solution)/shard_map/ppermute | solution.py:354
  196.6 26.3 %all-to-all-done.2 = bf16[64,24,1024]{2,1,0:T(8,128)(2,1)S(1)} async-done(((bf16[64,24,1024]{2,1,0:T(8,128)(2,1)}), bf16[64,24,1024]{2,1,0:T(8,128)(2,1)S(1)}, u32[]{:S(2)}, u32[]{:S(2)}) %all-to-all-start.2) | async-done | bytes 3145760 | tf_op jit(solution)/shard_map/all_to_all | solution.py:383
  222.9 1.1 copy-done.5
  224.0 1.5 token_sums.1
  225.5 1.0 collective-permute-start.3
  226.5 2.0 collective-permute-start.4
  228.6 0.0 collective-permute-done
  228.6 3.2 %collective-permute-start.5 = (bf16[48,1024]{1,0:T(8,128)(2,1)}, bf16[48,1024]{1,0:T(8,128)(2,1)S(1)}, u32[]{:S(2)}, u32[]{:S(2)}) collective-permute-start(bf16[48,1024]{1,0:T(8,128)(2,1)} %get-tuple-element.80), channel_id=1, source_target_pairs={{0,24},{8,0},{16,8},{24,16},{1,25},{9,1},{17,9},{25,17},{2,26},{10... | collective-permute-start | bytes 294920 | tf_op jit(solution)/shard_map/ppermute | solution.py:354
  231.7 0.0 collective-permute-done.1
  231.7 0.0 collective-permute-done.2
  231.7 1.1 fusion
  232.8 0.7 copy.14
  233.5 0.0 collective-permute-done.3
  233.5 1.5 collective-permute-done.4
  235.0 5.7 %collective-permute-done.5 = bf16[48,1024]{1,0:T(8,128)(2,1)S(1)} collective-permute-done((bf16[48,1024]{1,0:T(8,128)(2,1)}, bf16[48,1024]{1,0:T(8,128)(2,1)S(1)}, u32[]{:S(2)}, u32[]{:S(2)}) %collective-permute-start.5) | collective-permute-done | bytes 98336 | tf_op jit(solution)/shard_map/ppermute | solution.py:354
  240.7 0.1 add_convert_fusion
  240.8 0.7 pad_maximum_fusion
  (13 shorter events, 0.0 us)
Async XLA Ops:
  24.7 0.8 copy-start.12
  29.6 85.1 %copy-start = (bf16[1,2048,384]{2,1,0:T(8,128)(2,1)S(1)}, bf16[1,2048,384]{2,1,0:T(8,128)(2,1)}, u32[]{:S(2)}) copy-start(bf16[1,2048,384]{2,1,0:T(8,128)(2,1)} %param.13) | copy-start | bytes 4718596
  29.6 85.1 %copy-start.1 = (bf16[1,2048,384]{2,1,0:T(8,128)(2,1)S(1)}, bf16[1,2048,384]{2,1,0:T(8,128)(2,1)}, u32[]{:S(2)}) copy-start(bf16[1,2048,384]{2,1,0:T(8,128)(2,1)} %param.14) | copy-start | bytes 4718596
  29.6 85.1 %copy-start.3 = (bf16[1,384,2048]{2,1,0:T(8,128)(2,1)S(1)}, bf16[1,384,2048]{2,1,0:T(8,128)(2,1)}, u32[]{:S(2)}) copy-start(bf16[1,384,2048]{2,1,0:T(8,128)(2,1)} %param.15) | copy-start | bytes 4718596
  123.2 50.9 %all-to-all-start.1 = ((bf16[64,24,1024]{2,1,0:T(8,128)(2,1)}), bf16[64,24,1024]{2,1,0:T(8,128)(2,1)}, u32[]{:S(2)}, u32[]{:S(2)}) async-start(bf16[64,24,1024]{2,1,0:T(8,128)(2,1)} %bitcast.25), calls=%async_computation.1 | async-start | bytes 6291456 | tf_op jit(solution)/shard_map/all_to_all | solution.py:383
  134.9 0.8 copy-start.8
  135.8 0.8 copy-start.10
  136.5 1.4 copy-start.2
  137.9 13.6 %copy-start.4 = (bf16[192,1536]{1,0:T(8,128)(2,1)}, bf16[192,1536]{1,0:T(8,128)(2,1)S(1)}, u32[]{:S(2)}) copy-start(bf16[192,1536]{1,0:T(8,128)(2,1)S(1)} %get-tuple-element.76.mask_ref) | copy-start | bytes 1769476
  137.9 13.6 %copy-start.6 = (bf16[192,1536]{1,0:T(8,128)(2,1)}, bf16[192,1536]{1,0:T(8,128)(2,1)S(1)}, u32[]{:S(2)}) copy-start(bf16[192,1536]{1,0:T(8,128)(2,1)S(1)} %get-tuple-element.68.high_ref) | copy-start | bytes 1769476
  174.1 7.9 %copy-start.13 = (f32[64,128]{1,0:T(8,128)S(1)}, f32[64,128]{1,0:T(8,128)}, u32[]{:S(2)}) copy-start(f32[64,128]{1,0:T(8,128)} %get-tuple-element.46.expert_ref) | copy-start | bytes 98308
  174.1 48.8 %all-to-all-start.2 = ((bf16[64,24,1024]{2,1,0:T(8,128)(2,1)}), bf16[64,24,1024]{2,1,0:T(8,128)(2,1)S(1)}, u32[]{:S(2)}, u32[]{:S(2)}) async-start(bf16[64,24,1024]{2,1,0:T(8,128)(2,1)} %bitcast.27), calls=%async_computation.2 | async-start | bytes 6291456 | tf_op jit(solution)/shard_map/all_to_all | solution.py:383
  182.0 1.1 copy-start.7
  183.1 1.1 copy-start.9
  184.1 1.0 copy-start.11
  190.4 38.2 %collective-permute-start = (bf16[48,1152]{1,0:T(8,128)(2,1)}, bf16[48,1152]{1,0:T(8,128)(2,1)}, u32[]{:S(2)}, u32[]{:S(2)}) collective-permute-start(bf16[48,1152]{1,0:T(8,128)(2,1)} %get-tuple-element.72), channel_id=1, source_target_pairs={{0,8},{8,16},{16,24},{24,0},{1,9},{9,17},{17,25},{25,1},{2,10},{10... | collective-permute-start | bytes 331784 | tf_op jit(solution)/shard_map/ppermute | solution.py:354
  191.1 40.6 %collective-permute-start.1 = (bf16[48,1152]{1,0:T(8,128)(2,1)}, bf16[48,1152]{1,0:T(8,128)(2,1)}, u32[]{:S(2)}, u32[]{:S(2)}) collective-permute-start(bf16[48,1152]{1,0:T(8,128)(2,1)} %get-tuple-element.73), channel_id=1, source_target_pairs={{0,16},{8,24},{16,0},{24,8},{1,17},{9,25},{17,1},{25,9},{2,18},{10... | collective-permute-start | bytes 331784 | tf_op jit(solution)/shard_map/ppermute | solution.py:354
  193.2 38.5 %collective-permute-start.2 = (bf16[48,1152]{1,0:T(8,128)(2,1)S(1)}, bf16[48,1152]{1,0:T(8,128)(2,1)}, u32[]{:S(2)}, u32[]{:S(2)}) collective-permute-start(bf16[48,1152]{1,0:T(8,128)(2,1)S(1)} %get-tuple-element.74), channel_id=1, source_target_pairs={{0,24},{8,0},{16,8},{24,16},{1,25},{9,1},{17,9},{25,17},{2,26},{10... | collective-permute-start | bytes 331784 | tf_op jit(solution)/shard_map/ppermute | solution.py:354
  222.9 1.1 copy-start.5
  225.5 8.0 %collective-permute-start.3 = (bf16[48,1024]{1,0:T(8,128)(2,1)}, bf16[48,1024]{1,0:T(8,128)(2,1)S(1)}, u32[]{:S(2)}, u32[]{:S(2)}) collective-permute-start(bf16[48,1024]{1,0:T(8,128)(2,1)} %get-tuple-element.78), channel_id=1, source_target_pairs={{0,8},{8,16},{16,24},{24,0},{1,9},{9,17},{17,25},{25,1},{2,10},{10... | collective-permute-start | bytes 294920 | tf_op jit(solution)/shard_map/ppermute | solution.py:354
  226.5 8.5 %collective-permute-start.4 = (bf16[48,1024]{1,0:T(8,128)(2,1)}, bf16[48,1024]{1,0:T(8,128)(2,1)S(1)}, u32[]{:S(2)}, u32[]{:S(2)}) collective-permute-start(bf16[48,1024]{1,0:T(8,128)(2,1)} %get-tuple-element.79), channel_id=1, source_target_pairs={{0,16},{8,24},{16,0},{24,8},{1,17},{9,25},{17,1},{25,9},{2,18},{10... | collective-permute-start | bytes 294920 | tf_op jit(solution)/shard_map/ppermute | solution.py:354
  228.6 12.2 %collective-permute-start.5 = (bf16[48,1024]{1,0:T(8,128)(2,1)}, bf16[48,1024]{1,0:T(8,128)(2,1)S(1)}, u32[]{:S(2)}, u32[]{:S(2)}) collective-permute-start(bf16[48,1024]{1,0:T(8,128)(2,1)} %get-tuple-element.80), channel_id=1, source_target_pairs={{0,24},{8,0},{16,8},{24,16},{1,25},{9,1},{17,9},{25,17},{2,26},{10... | collective-permute-start | bytes 294920 | tf_op jit(solution)/shard_map/ppermute | solution.py:354

commit v3 on v2

--- a/solution.py
+++ b/solution.py
@@ -10,7 +10,7 @@
 
 BF = jnp.bfloat16
 F32 = jnp.float32
-SPREAD = ("zlo", "x", "y", "core")
+SPREAD = ("y", "core", "zlo", "x")
 EXTRA = 128
 STEPS = (0, 1, 2, 3)
 INNER = (((0,), (0,)), ((), ()))
@@ -63,11 +63,11 @@
 def dest_experts(index, slot_map, dests):
     groups, members = slot_map.shape
     near = dests // groups
-    row = (iota((dests, groups), 0) % groups == iota((dests, groups), 1)).astype(BF)
+    row = (iota((dests, groups), 0) // near == iota((dests, groups), 1)).astype(BF)
     held = jnp.dot(row, slot_map.astype(F32).astype(BF), preferred_element_type=F32)
-    column = index * near + iota((dests, members), 0) // groups
+    column = index * near + iota((dests, members), 0) % near
     held = jnp.sum(jnp.where(iota((dests, members), 1) == column, held, 0.0), axis=1, keepdims=True)
-    first = iota((dests, 1), 0) % groups * (members // 2)
+    first = iota((dests, 1), 0) // near * (members // 2)
     return (held.astype(jnp.int32) // 2 + first).astype(F32)
 
 

time: 244 us -> 238 us (0.975)
  starting transfers between devices: 31.4 us -> 25.5 us
    all_to_all x2, starting transfers between devices: 19 us -> 10.9 us  [exchange(): lax.all_to_all(rows.reshape(dests, slots, columns), SPREAD, split_axis=0,...]
    all_to_all x2, waiting for transfers between devices: 41.1 us -> 43.8 us  [exchange(): lax.all_to_all(rows.reshape(dests, slots, columns), SPREAD, split_axis=0,...]
where the time goes in v3:
time: 238 us; the launch traced here: 237 us
  blocking collectives  108 us (45%)
  waiting for transfers between devices  49.5 us (21%)
  Pallas kernels  43.2 us (18%)
  starting transfers between devices  25.5 us (11%)
  local copies, waits for them, and re-layouts  8.63 us (4%)
    all_to_all x1, blocking collectives, exchange(): lax.all_to_all(rows.reshape(dests, slots, columns), SPREAD, split_axis=0,...  85.7 us
    all_to_all x2, waiting for transfers between devices, exchange(): lax.all_to_all(rows.reshape(dests, slots, columns), SPREAD, split_axis=0,...  43.8 us
    all_gather x1, blocking collectives, body(): rows = lax.all_gather(own, 'zhi', axis=0, tiled=True)  22.2 us
    pallas_call x2, Pallas kernels, expert_call(): pl.pallas_call(functools.partial(kernel, slots), grid=(steps,), in_specs=...  22.1 us
    ppermute x6, starting transfers between devices, send_blocks(): lax.ppermute(rows, 'zhi', [(i, (i + step) % n) for i in range(n)])  14.7 us
    all_to_all x2, starting transfers between devices, exchange(): lax.all_to_all(rows.reshape(dests, slots, columns), SPREAD, split_axis=0,...  10.9 us
    unnamed x29, local copies, waits for them, and re-layouts  8.61 us
    pallas_call x1, Pallas kernels, slab_grads(): pl.pallas_call(functools.partial(slab_grad_kernel, slots), grid=(steps,),...  7.74 us
  transfers between devices with their start and end apart: 8, of which 4 were waited for; matrix products, arithmetic and copies ran while one was open for 1% of the time, Pallas kernels for 12%

profile of v3, /device:TPU:1, one launch (start us, length us, event | category | flops | bytes accessed | tf_op | source)
XLA Modules:
  0.0 237.4 jit_solution(1185448556553375254)
XLA Ops:
  0.6 1.9 pack.1
  2.5 22.2 %all_gather.3.rows_ref = bf16[192,2176]{1,0:T(8,128)(2,1)S(1)} all-gather(bf16[48,2176]{1,0:T(8,128)(2,1)} %get-tuple-element.45), channel_id=1, replica_groups=mesh['y'=4,'core'=2,'zhi'=4,'zlo'=2,'x'=4] {'zhi'}, dimensions={0}, use_global_device_ids=true | all-gather | bytes 1044480 | tf_op jit(solution)/shard_map/all_gather | solution.py:379
  24.7 0.0 copy-start.12
  24.7 0.8 copy-done.12
  25.5 4.1 %fill.1 = (bf16[1536,2048]{1,0:T(8,128)(2,1)}, f32[64,192]{1,0:T(8,128)S(1)}, f32[64,192]{1,0:T(8,128)S(1)}, f32[8,192]{1,0:T(8,128)S(1)}) custom-call(bf16[192,2176]{1,0:T(8,128)(2,1)S(1)} %all_gather.3.rows_ref, f32[64,128]{1,0:T(8,128)S(1)} %copy-done.12), custom_call_target="tpu_custom_call" | custom-call | flops 1207959552 | bytes 6291456 | tf_op jit(solution)/shard_map/fill/pallas_call | solution.py:129
  29.6 0.0 copy-start
  29.6 85.7 %all_to_all.15 = bf16[64,24,2048]{2,1,0:T(8,128)(2,1)} all-to-all(bf16[64,24,2048]{2,1,0:T(8,128)(2,1)} %bitcast.26), channel_id=1, replica_groups=mesh['y'=4,'core'=2,'zhi'=4,'zlo'=2,'x'=4] {'y','core','zlo','x'}, dimensions={0} | all-to-all | bytes 12582912 | tf_op jit(solution)/shard_map/all_to_all | solution.py:383
  115.3 0.0 copy-done
  115.3 0.0 copy-done.1
  115.3 0.0 copy-done.3
  115.3 8.5 %forward.1 = bf16[1536,1024]{1,0:T(8,128)(2,1)} custom-call(bf16[1536,2048]{1,0:T(8,128)(2,1)} %bitcast.22, bf16[2048,384]{1,0:T(8,128)(2,1)S(1)} %bitcast.16, bf16[2048,384]{1,0:T(8,128)(2,1)S(1)} %bitcast.18, bf16[384,2048]{1,0:T(8,128)(2,1)S(1)} %bitcast.21), custom_call_target="tpu_custom_call" | custom-call | flops 3623878656 | bytes 14155776 | tf_op jit(solution)/shard_map/forward/pallas_call | solution.py:192
  123.8 5.6 %all-to-all-start.1 = ((bf16[64,24,1024]{2,1,0:T(8,128)(2,1)}), bf16[64,24,1024]{2,1,0:T(8,128)(2,1)}, u32[]{:S(2)}, u32[]{:S(2)}) async-start(bf16[64,24,1024]{2,1,0:T(8,128)(2,1)} %bitcast.25), calls=%async_computation.1 | async-start | bytes 6291456 | tf_op jit(solution)/shard_map/all_to_all | solution.py:383
  129.5 0.7 prepare.1
  130.2 0.0 copy-start.8
  130.2 0.8 copy-done.8
  131.0 0.8 copy-done.10
  131.8 1.4 copy-done.2
  133.2 13.6 %backward.1 = (bf16[1536,1024]{1,0:T(8,128)(2,1)}, bf16[768,384]{1,0:T(8,128)(2,1)S(1)}, bf16[768,384]{1,0:T(8,128)(2,1)S(1)}, bf16[768,384]{1,0:T(8,128)(2,1)S(1)}) custom-call(bf16[1536,2048]{1,0:T(8,128)(2,1)} %bitcast.23, bf16[2048,384]{1,0:T(8,128)(2,1)S(1)} %bitcast.17, bf16[2048,384]{1,0:T(8,128)(2,1)S(1)} %bitcast.19, bf16[384,2048]{1,0:T(8,128)(2,1)} %bitcast.20), custom_call_target="tpu_custom_call" | custom-call | flops 3623878656 | bytes 14155776 | tf_op jit(solution)/shard_map/backward/pallas_call | solution.py:192
  146.8 0.0 copy-done.4
  146.8 0.0 copy-done.6
  146.8 7.7 %slab_grads.1 = (bf16[2048,384]{1,0:T(8,128)(2,1)}, bf16[2048,384]{1,0:T(8,128)(2,1)}, bf16[384,2048]{1,0:T(8,128)(2,1)}) custom-call(bf16[1536,2048]{1,0:T(8,128)(2,1)} %bitcast.24, bf16[768,384]{1,0:T(8,128)(2,1)S(1)} %get-tuple-element.58.hidden_ref, bf16[768,384]{1,0:T(8,128)(2,1)S(1)} %get-tuple-element.59.gate_grad_ref, ...), custom_call_target="tpu_custom_call" | custom-call | flops 3623878656 | bytes 11010048 | tf_op jit(solution)/shard_map/slab_grads/pallas_call | solution.py:216
  154.5 15.8 %all-to-all-done.1 = bf16[64,24,1024]{2,1,0:T(8,128)(2,1)} async-done(((bf16[64,24,1024]{2,1,0:T(8,128)(2,1)}), bf16[64,24,1024]{2,1,0:T(8,128)(2,1)}, u32[]{:S(2)}, u32[]{:S(2)}) %all-to-all-start.1) | async-done | bytes 3145760 | tf_op jit(solution)/shard_map/all_to_all | solution.py:383
  170.3 5.2 %all-to-all-start.2 = ((bf16[64,24,1024]{2,1,0:T(8,128)(2,1)}), bf16[64,24,1024]{2,1,0:T(8,128)(2,1)S(1)}, u32[]{:S(2)}, u32[]{:S(2)}) async-start(bf16[64,24,1024]{2,1,0:T(8,128)(2,1)} %bitcast.27), calls=%async_computation.2 | async-start | bytes 6291456 | tf_op jit(solution)/shard_map/all_to_all | solution.py:383
  175.5 0.0 copy-done.13
  175.5 0.0 copy-start.7
  175.5 1.1 copy-done.7
  176.6 1.1 copy-done.9
  177.7 1.0 copy-done.11
  178.7 5.3 %layer_sums.1 = (bf16[48,1152]{1,0:T(8,128)(2,1)S(1)}, bf16[48,1152]{1,0:T(8,128)(2,1)}, bf16[48,1152]{1,0:T(8,128)(2,1)}, bf16[48,1152]{1,0:T(8,128)(2,1)S(1)}) custom-call(s32[1,1]{1,0:T(1,128)} %bitcast.index_ref, bf16[1536,1024]{1,0:T(8,128)(2,1)} %bitcast.9.back_ref, bf16[192,1024]{1,0:T(8,128)(2,1)S(1)} %copy-done.11, ...), custom_call_target="tpu_custom_call" | custom-call | flops 1811939328 | bytes 3145728 | tf_op jit(solution)/shard_map/layer_sums/pallas_call | solution.py:308
  183.9 0.7 collective-permute-start
  184.7 2.1 collective-permute-start.1
  186.7 3.4 %collective-permute-start.2 = (bf16[48,1152]{1,0:T(8,128)(2,1)S(1)}, bf16[48,1152]{1,0:T(8,128)(2,1)}, u32[]{:S(2)}, u32[]{:S(2)}) collective-permute-start(bf16[48,1152]{1,0:T(8,128)(2,1)S(1)} %get-tuple-element.74), channel_id=1, source_target_pairs={{0,24},{8,0},{16,8},{24,16},{1,25},{9,1},{17,9},{25,17},{2,26},{10... | collective-permute-start | bytes 331784 | tf_op jit(solution)/shard_map/ppermute | solution.py:354
  190.2 28.1 %all-to-all-done.2 = bf16[64,24,1024]{2,1,0:T(8,128)(2,1)S(1)} async-done(((bf16[64,24,1024]{2,1,0:T(8,128)(2,1)}), bf16[64,24,1024]{2,1,0:T(8,128)(2,1)S(1)}, u32[]{:S(2)}, u32[]{:S(2)}) %all-to-all-start.2) | async-done | bytes 3145760 | tf_op jit(solution)/shard_map/all_to_all | solution.py:383
  218.2 1.1 copy-done.5
  219.3 1.5 token_sums.1
  220.8 0.2 collective-permute-start.3
  221.0 4.6 %collective-permute-start.4 = (bf16[48,1024]{1,0:T(8,128)(2,1)}, bf16[48,1024]{1,0:T(8,128)(2,1)S(1)}, u32[]{:S(2)}, u32[]{:S(2)}) collective-permute-start(bf16[48,1024]{1,0:T(8,128)(2,1)} %get-tuple-element.79), channel_id=1, source_target_pairs={{0,16},{8,24},{16,0},{24,8},{1,17},{9,25},{17,1},{25,9},{2,18},{10... | collective-permute-start | bytes 294920 | tf_op jit(solution)/shard_map/ppermute | solution.py:354
  225.6 0.0 collective-permute-done
  225.7 3.6 %collective-permute-start.5 = (bf16[48,1024]{1,0:T(8,128)(2,1)}, bf16[48,1024]{1,0:T(8,128)(2,1)S(1)}, u32[]{:S(2)}, u32[]{:S(2)}) collective-permute-start(bf16[48,1024]{1,0:T(8,128)(2,1)} %get-tuple-element.80), channel_id=1, source_target_pairs={{0,24},{8,0},{16,8},{24,16},{1,25},{9,1},{17,9},{25,17},{2,26},{10... | collective-permute-start | bytes 294920 | tf_op jit(solution)/shard_map/ppermute | solution.py:354
  229.2 0.0 collective-permute-done.1
  229.2 0.0 collective-permute-done.2
  229.2 1.1 fusion
  230.3 0.7 copy.14
  231.0 0.0 collective-permute-done.3
  231.0 1.3 collective-permute-done.4
  232.3 4.3 %collective-permute-done.5 = bf16[48,1024]{1,0:T(8,128)(2,1)S(1)} collective-permute-done((bf16[48,1024]{1,0:T(8,128)(2,1)}, bf16[48,1024]{1,0:T(8,128)(2,1)S(1)}, u32[]{:S(2)}, u32[]{:S(2)}) %collective-permute-start.5) | collective-permute-done | bytes 98336 | tf_op jit(solution)/shard_map/ppermute | solution.py:354
  236.6 0.1 add_convert_fusion
  236.7 0.7 pad_maximum_fusion
  (13 shorter events, 0.0 us)
Async XLA Ops:
  24.7 0.8 copy-start.12
  29.6 85.7 %copy-start = (bf16[1,2048,384]{2,1,0:T(8,128)(2,1)S(1)}, bf16[1,2048,384]{2,1,0:T(8,128)(2,1)}, u32[]{:S(2)}) copy-start(bf16[1,2048,384]{2,1,0:T(8,128)(2,1)} %param.13) | copy-start | bytes 4718596
  29.6 85.7 %copy-start.1 = (bf16[1,2048,384]{2,1,0:T(8,128)(2,1)S(1)}, bf16[1,2048,384]{2,1,0:T(8,128)(2,1)}, u32[]{:S(2)}) copy-start(bf16[1,2048,384]{2,1,0:T(8,128)(2,1)} %param.14) | copy-start | bytes 4718596
  29.6 85.7 %copy-start.3 = (bf16[1,384,2048]{2,1,0:T(8,128)(2,1)S(1)}, bf16[1,384,2048]{2,1,0:T(8,128)(2,1)}, u32[]{:S(2)}) copy-start(bf16[1,384,2048]{2,1,0:T(8,128)(2,1)} %param.15) | copy-start | bytes 4718596
  123.8 46.4 %all-to-all-start.1 = ((bf16[64,24,1024]{2,1,0:T(8,128)(2,1)}), bf16[64,24,1024]{2,1,0:T(8,128)(2,1)}, u32[]{:S(2)}, u32[]{:S(2)}) async-start(bf16[64,24,1024]{2,1,0:T(8,128)(2,1)} %bitcast.25), calls=%async_computation.1 | async-start | bytes 6291456 | tf_op jit(solution)/shard_map/all_to_all | solution.py:383
  130.2 0.8 copy-start.8
  131.0 0.8 copy-start.10
  131.8 1.4 copy-start.2
  133.2 13.6 %copy-start.4 = (bf16[192,1536]{1,0:T(8,128)(2,1)}, bf16[192,1536]{1,0:T(8,128)(2,1)S(1)}, u32[]{:S(2)}) copy-start(bf16[192,1536]{1,0:T(8,128)(2,1)S(1)} %get-tuple-element.76.mask_ref) | copy-start | bytes 1769476
  133.2 13.6 %copy-start.6 = (bf16[192,1536]{1,0:T(8,128)(2,1)}, bf16[192,1536]{1,0:T(8,128)(2,1)S(1)}, u32[]{:S(2)}) copy-start(bf16[192,1536]{1,0:T(8,128)(2,1)S(1)} %get-tuple-element.68.high_ref) | copy-start | bytes 1769476
  170.3 5.3 %copy-start.13 = (f32[64,128]{1,0:T(8,128)S(1)}, f32[64,128]{1,0:T(8,128)}, u32[]{:S(2)}) copy-start(f32[64,128]{1,0:T(8,128)} %get-tuple-element.46.expert_ref) | copy-start | bytes 98308
  170.3 48.0 %all-to-all-start.2 = ((bf16[64,24,1024]{2,1,0:T(8,128)(2,1)}), bf16[64,24,1024]{2,1,0:T(8,128)(2,1)S(1)}, u32[]{:S(2)}, u32[]{:S(2)}) async-start(bf16[64,24,1024]{2,1,0:T(8,128)(2,1)} %bitcast.27), calls=%async_computation.2 | async-start | bytes 6291456 | tf_op jit(solution)/shard_map/all_to_all | solution.py:383
  175.5 1.1 copy-start.7
  176.6 1.1 copy-start.9
  177.7 1.0 copy-start.11
  183.9 41.7 %collective-permute-start = (bf16[48,1152]{1,0:T(8,128)(2,1)}, bf16[48,1152]{1,0:T(8,128)(2,1)}, u32[]{:S(2)}, u32[]{:S(2)}) collective-permute-start(bf16[48,1152]{1,0:T(8,128)(2,1)} %get-tuple-element.72), channel_id=1, source_target_pairs={{0,8},{8,16},{16,24},{24,0},{1,9},{9,17},{17,25},{25,1},{2,10},{10... | collective-permute-start | bytes 331784 | tf_op jit(solution)/shard_map/ppermute | solution.py:354
  184.7 44.6 %collective-permute-start.1 = (bf16[48,1152]{1,0:T(8,128)(2,1)}, bf16[48,1152]{1,0:T(8,128)(2,1)}, u32[]{:S(2)}, u32[]{:S(2)}) collective-permute-start(bf16[48,1152]{1,0:T(8,128)(2,1)} %get-tuple-element.73), channel_id=1, source_target_pairs={{0,16},{8,24},{16,0},{24,8},{1,17},{9,25},{17,1},{25,9},{2,18},{10... | collective-permute-start | bytes 331784 | tf_op jit(solution)/shard_map/ppermute | solution.py:354
  186.7 42.5 %collective-permute-start.2 = (bf16[48,1152]{1,0:T(8,128)(2,1)S(1)}, bf16[48,1152]{1,0:T(8,128)(2,1)}, u32[]{:S(2)}, u32[]{:S(2)}) collective-permute-start(bf16[48,1152]{1,0:T(8,128)(2,1)S(1)} %get-tuple-element.74), channel_id=1, source_target_pairs={{0,24},{8,0},{16,8},{24,16},{1,25},{9,1},{17,9},{25,17},{2,26},{10... | collective-permute-start | bytes 331784 | tf_op jit(solution)/shard_map/ppermute | solution.py:354
  218.2 1.1 copy-start.5
  220.8 10.2 %collective-permute-start.3 = (bf16[48,1024]{1,0:T(8,128)(2,1)}, bf16[48,1024]{1,0:T(8,128)(2,1)S(1)}, u32[]{:S(2)}, u32[]{:S(2)}) collective-permute-start(bf16[48,1024]{1,0:T(8,128)(2,1)} %get-tuple-element.78), channel_id=1, source_target_pairs={{0,8},{8,16},{16,24},{24,0},{1,9},{9,17},{17,25},{25,1},{2,10},{10... | collective-permute-start | bytes 294920 | tf_op jit(solution)/shard_map/ppermute | solution.py:354
  221.0 11.3 %collective-permute-start.4 = (bf16[48,1024]{1,0:T(8,128)(2,1)}, bf16[48,1024]{1,0:T(8,128)(2,1)S(1)}, u32[]{:S(2)}, u32[]{:S(2)}) collective-permute-start(bf16[48,1024]{1,0:T(8,128)(2,1)} %get-tuple-element.79), channel_id=1, source_target_pairs={{0,16},{8,24},{16,0},{24,8},{1,17},{9,25},{17,1},{25,9},{2,18},{10... | collective-permute-start | bytes 294920 | tf_op jit(solution)/shard_map/ppermute | solution.py:354
  225.7 11.0 %collective-permute-start.5 = (bf16[48,1024]{1,0:T(8,128)(2,1)}, bf16[48,1024]{1,0:T(8,128)(2,1)S(1)}, u32[]{:S(2)}, u32[]{:S(2)}) collective-permute-start(bf16[48,1024]{1,0:T(8,128)(2,1)} %get-tuple-element.80), channel_id=1, source_target_pairs={{0,24},{8,0},{16,8},{24,16},{1,25},{9,1},{17,9},{25,17},{2,26},{10... | collective-permute-start | bytes 294920 | tf_op jit(solution)/shard_map/ppermute | solution.py:354

commit v4 on v3

--- a/solution.py
+++ b/solution.py
@@ -12,7 +12,7 @@
 F32 = jnp.float32
 SPREAD = ("y", "core", "zlo", "x")
 EXTRA = 128
-STEPS = (0, 1, 2, 3)
+STEPS = (0, 2, 1, 3)
 INNER = (((0,), (0,)), ((), ()))
 OUTER = (((1,), (1,)), ((), ()))
 VMEM_LIMIT = 48 * 1024 * 1024

time: 238 us -> 237 us (level)
  no operation moved by 1% of the time
where the time goes in v4:
time: 237 us; the launch traced here: 236 us
  blocking collectives  108 us (46%)
  waiting for transfers between devices  48.6 us (21%)
  Pallas kernels  43.2 us (18%)
  starting transfers between devices  25.1 us (11%)
  local copies, waits for them, and re-layouts  8.63 us (4%)
    all_to_all x1, blocking collectives, exchange(): lax.all_to_all(rows.reshape(dests, slots, columns), SPREAD, split_axis=0,...  85.7 us
    all_to_all x2, waiting for transfers between devices, exchange(): lax.all_to_all(rows.reshape(dests, slots, columns), SPREAD, split_axis=0,...  44.2 us
    all_gather x1, blocking collectives, body(): rows = lax.all_gather(own, 'zhi', axis=0, tiled=True)  22.2 us
    pallas_call x2, Pallas kernels, expert_call(): pl.pallas_call(functools.partial(kernel, slots), grid=(steps,), in_specs=...  22.1 us
    ppermute x6, starting transfers between devices, send_blocks(): lax.ppermute(rows, 'zhi', [(i, (i + step) % n) for i in range(n)])  14.3 us
    all_to_all x2, starting transfers between devices, exchange(): lax.all_to_all(rows.reshape(dests, slots, columns), SPREAD, split_axis=0,...  10.9 us
    unnamed x29, local copies, waits for them, and re-layouts  8.61 us
    pallas_call x1, Pallas kernels, slab_grads(): pl.pallas_call(functools.partial(slab_grad_kernel, slots), grid=(steps,),...  7.74 us
  transfers between devices with their start and end apart: 8, of which 4 were waited for; matrix products, arithmetic and copies ran while one was open for 1% of the time, Pallas kernels for 12%

profile of v4, /device:TPU:1, one launch (start us, length us, event | category | flops | bytes accessed | tf_op | source)
XLA Modules:
  0.0 236.2 jit_solution(15338305680891178164)
XLA Ops:
  0.6 1.9 pack.1
  2.5 22.2 %all_gather.3.rows_ref = bf16[192,2176]{1,0:T(8,128)(2,1)S(1)} all-gather(bf16[48,2176]{1,0:T(8,128)(2,1)} %get-tuple-element.45), channel_id=1, replica_groups=mesh['y'=4,'core'=2,'zhi'=4,'zlo'=2,'x'=4] {'zhi'}, dimensions={0}, use_global_device_ids=true | all-gather | bytes 1044480 | tf_op jit(solution)/shard_map/all_gather | solution.py:379
  24.7 0.0 copy-start.12
  24.7 0.8 copy-done.12
  25.5 4.1 %fill.1 = (bf16[1536,2048]{1,0:T(8,128)(2,1)}, f32[64,192]{1,0:T(8,128)S(1)}, f32[64,192]{1,0:T(8,128)S(1)}, f32[8,192]{1,0:T(8,128)S(1)}) custom-call(bf16[192,2176]{1,0:T(8,128)(2,1)S(1)} %all_gather.3.rows_ref, f32[64,128]{1,0:T(8,128)S(1)} %copy-done.12), custom_call_target="tpu_custom_call" | custom-call | flops 1207959552 | bytes 6291456 | tf_op jit(solution)/shard_map/fill/pallas_call | solution.py:129
  29.6 0.0 copy-start
  29.6 85.7 %all_to_all.15 = bf16[64,24,2048]{2,1,0:T(8,128)(2,1)} all-to-all(bf16[64,24,2048]{2,1,0:T(8,128)(2,1)} %bitcast.26), channel_id=1, replica_groups=mesh['y'=4,'core'=2,'zhi'=4,'zlo'=2,'x'=4] {'y','core','zlo','x'}, dimensions={0} | all-to-all | bytes 12582912 | tf_op jit(solution)/shard_map/all_to_all | solution.py:383
  115.3 0.0 copy-done
  115.3 0.0 copy-done.1
  115.3 0.0 copy-done.3
  115.3 8.5 %forward.1 = bf16[1536,1024]{1,0:T(8,128)(2,1)} custom-call(bf16[1536,2048]{1,0:T(8,128)(2,1)} %bitcast.22, bf16[2048,384]{1,0:T(8,128)(2,1)S(1)} %bitcast.16, bf16[2048,384]{1,0:T(8,128)(2,1)S(1)} %bitcast.18, bf16[384,2048]{1,0:T(8,128)(2,1)S(1)} %bitcast.21), custom_call_target="tpu_custom_call" | custom-call | flops 3623878656 | bytes 14155776 | tf_op jit(solution)/shard_map/forward/pallas_call | solution.py:192
  123.8 5.6 %all-to-all-start.1 = ((bf16[64,24,1024]{2,1,0:T(8,128)(2,1)}), bf16[64,24,1024]{2,1,0:T(8,128)(2,1)}, u32[]{:S(2)}, u32[]{:S(2)}) async-start(bf16[64,24,1024]{2,1,0:T(8,128)(2,1)} %bitcast.25), calls=%async_computation.1 | async-start | bytes 6291456 | tf_op jit(solution)/shard_map/all_to_all | solution.py:383
  129.5 0.7 prepare.1
  130.2 0.0 copy-start.8
  130.2 0.8 copy-done.8
  131.0 0.8 copy-done.10
  131.8 1.4 copy-done.2
  133.2 13.6 %backward.1 = (bf16[1536,1024]{1,0:T(8,128)(2,1)}, bf16[768,384]{1,0:T(8,128)(2,1)S(1)}, bf16[768,384]{1,0:T(8,128)(2,1)S(1)}, bf16[768,384]{1,0:T(8,128)(2,1)S(1)}) custom-call(bf16[1536,2048]{1,0:T(8,128)(2,1)} %bitcast.23, bf16[2048,384]{1,0:T(8,128)(2,1)S(1)} %bitcast.17, bf16[2048,384]{1,0:T(8,128)(2,1)S(1)} %bitcast.19, bf16[384,2048]{1,0:T(8,128)(2,1)} %bitcast.20), custom_call_target="tpu_custom_call" | custom-call | flops 3623878656 | bytes 14155776 | tf_op jit(solution)/shard_map/backward/pallas_call | solution.py:192
  146.8 0.0 copy-done.4
  146.8 0.0 copy-done.6
  146.8 7.7 %slab_grads.1 = (bf16[2048,384]{1,0:T(8,128)(2,1)}, bf16[2048,384]{1,0:T(8,128)(2,1)}, bf16[384,2048]{1,0:T(8,128)(2,1)}) custom-call(bf16[1536,2048]{1,0:T(8,128)(2,1)} %bitcast.24, bf16[768,384]{1,0:T(8,128)(2,1)S(1)} %get-tuple-element.58.hidden_ref, bf16[768,384]{1,0:T(8,128)(2,1)S(1)} %get-tuple-element.59.gate_grad_ref, ...), custom_call_target="tpu_custom_call" | custom-call | flops 3623878656 | bytes 11010048 | tf_op jit(solution)/shard_map/slab_grads/pallas_call | solution.py:216
  154.5 15.8 %all-to-all-done.1 = bf16[64,24,1024]{2,1,0:T(8,128)(2,1)} async-done(((bf16[64,24,1024]{2,1,0:T(8,128)(2,1)}), bf16[64,24,1024]{2,1,0:T(8,128)(2,1)}, u32[]{:S(2)}, u32[]{:S(2)}) %all-to-all-start.1) | async-done | bytes 3145760 | tf_op jit(solution)/shard_map/all_to_all | solution.py:383
  170.3 5.2 %all-to-all-start.2 = ((bf16[64,24,1024]{2,1,0:T(8,128)(2,1)}), bf16[64,24,1024]{2,1,0:T(8,128)(2,1)S(1)}, u32[]{:S(2)}, u32[]{:S(2)}) async-start(bf16[64,24,1024]{2,1,0:T(8,128)(2,1)} %bitcast.27), calls=%async_computation.2 | async-start | bytes 6291456 | tf_op jit(solution)/shard_map/all_to_all | solution.py:383
  175.5 0.0 copy-done.13
  175.5 0.0 copy-start.7
  175.5 1.1 copy-done.7
  176.6 1.1 copy-done.9
  177.7 1.0 copy-done.11
  178.7 5.3 %layer_sums.1 = (bf16[48,1152]{1,0:T(8,128)(2,1)S(1)}, bf16[48,1152]{1,0:T(8,128)(2,1)}, bf16[48,1152]{1,0:T(8,128)(2,1)}, bf16[48,1152]{1,0:T(8,128)(2,1)S(1)}) custom-call(s32[1,1]{1,0:T(1,128)} %bitcast.index_ref, bf16[1536,1024]{1,0:T(8,128)(2,1)} %bitcast.9.back_ref, bf16[192,1024]{1,0:T(8,128)(2,1)S(1)} %copy-done.11, ...), custom_call_target="tpu_custom_call" | custom-call | flops 1811939328 | bytes 3145728 | tf_op jit(solution)/shard_map/layer_sums/pallas_call | solution.py:308
  183.9 2.7 %collective-permute-start = (bf16[48,1152]{1,0:T(8,128)(2,1)}, bf16[48,1152]{1,0:T(8,128)(2,1)}, u32[]{:S(2)}, u32[]{:S(2)}) collective-permute-start(bf16[48,1152]{1,0:T(8,128)(2,1)} %get-tuple-element.72), channel_id=1, source_target_pairs={{0,16},{8,24},{16,0},{24,8},{1,17},{9,25},{17,1},{25,9},{2,18},{10... | collective-permute-start | bytes 331784 | tf_op jit(solution)/shard_map/ppermute | solution.py:354
  186.6 0.2 collective-permute-start.1
  186.7 3.4 %collective-permute-start.2 = (bf16[48,1152]{1,0:T(8,128)(2,1)S(1)}, bf16[48,1152]{1,0:T(8,128)(2,1)}, u32[]{:S(2)}, u32[]{:S(2)}) collective-permute-start(bf16[48,1152]{1,0:T(8,128)(2,1)S(1)} %get-tuple-element.74), channel_id=1, source_target_pairs={{0,24},{8,0},{16,8},{24,16},{1,25},{9,1},{17,9},{25,17},{2,26},{10... | collective-permute-start | bytes 331784 | tf_op jit(solution)/shard_map/ppermute | solution.py:354
  190.2 28.5 %all-to-all-done.2 = bf16[64,24,1024]{2,1,0:T(8,128)(2,1)S(1)} async-done(((bf16[64,24,1024]{2,1,0:T(8,128)(2,1)}), bf16[64,24,1024]{2,1,0:T(8,128)(2,1)S(1)}, u32[]{:S(2)}, u32[]{:S(2)}) %all-to-all-start.2) | async-done | bytes 3145760 | tf_op jit(solution)/shard_map/all_to_all | solution.py:383
  218.6 1.1 copy-done.5
  219.7 1.5 token_sums.1
  221.2 4.4 %collective-permute-start.3 = (bf16[48,1024]{1,0:T(8,128)(2,1)}, bf16[48,1024]{1,0:T(8,128)(2,1)S(1)}, u32[]{:S(2)}, u32[]{:S(2)}) collective-permute-start(bf16[48,1024]{1,0:T(8,128)(2,1)} %get-tuple-element.78), channel_id=1, source_target_pairs={{0,16},{8,24},{16,0},{24,8},{1,17},{9,25},{17,1},{25,9},{2,18},{10... | collective-permute-start | bytes 294920 | tf_op jit(solution)/shard_map/ppermute | solution.py:354
  225.6 0.0 collective-permute-start.4
  225.6 0.0 collective-permute-done
  225.7 3.6 %collective-permute-start.5 = (bf16[48,1024]{1,0:T(8,128)(2,1)}, bf16[48,1024]{1,0:T(8,128)(2,1)S(1)}, u32[]{:S(2)}, u32[]{:S(2)}) collective-permute-start(bf16[48,1024]{1,0:T(8,128)(2,1)} %get-tuple-element.80), channel_id=1, source_target_pairs={{0,24},{8,0},{16,8},{24,16},{1,25},{9,1},{17,9},{25,17},{2,26},{10... | collective-permute-start | bytes 294920 | tf_op jit(solution)/shard_map/ppermute | solution.py:354
  229.2 0.0 collective-permute-done.1
  229.2 0.0 collective-permute-done.2
  229.2 1.1 fusion
  230.3 0.7 copy.14
  231.0 1.7 collective-permute-done.3
  232.7 2.7 %collective-permute-done.4 = bf16[48,1024]{1,0:T(8,128)(2,1)S(1)} collective-permute-done((bf16[48,1024]{1,0:T(8,128)(2,1)}, bf16[48,1024]{1,0:T(8,128)(2,1)S(1)}, u32[]{:S(2)}, u32[]{:S(2)}) %collective-permute-start.4) | collective-permute-done | bytes 98336 | tf_op jit(solution)/shard_map/ppermute | solution.py:354
  235.4 0.0 collective-permute-done.5
  235.4 0.1 add_convert_fusion
  235.5 0.7 pad_maximum_fusion
  (13 shorter events, 0.0 us)
Async XLA Ops:
  24.7 0.8 copy-start.12
  29.6 85.7 %copy-start = (bf16[1,2048,384]{2,1,0:T(8,128)(2,1)S(1)}, bf16[1,2048,384]{2,1,0:T(8,128)(2,1)}, u32[]{:S(2)}) copy-start(bf16[1,2048,384]{2,1,0:T(8,128)(2,1)} %param.13) | copy-start | bytes 4718596
  29.6 85.7 %copy-start.1 = (bf16[1,2048,384]{2,1,0:T(8,128)(2,1)S(1)}, bf16[1,2048,384]{2,1,0:T(8,128)(2,1)}, u32[]{:S(2)}) copy-start(bf16[1,2048,384]{2,1,0:T(8,128)(2,1)} %param.14) | copy-start | bytes 4718596
  29.6 85.7 %copy-start.3 = (bf16[1,384,2048]{2,1,0:T(8,128)(2,1)S(1)}, bf16[1,384,2048]{2,1,0:T(8,128)(2,1)}, u32[]{:S(2)}) copy-start(bf16[1,384,2048]{2,1,0:T(8,128)(2,1)} %param.15) | copy-start | bytes 4718596
  123.8 46.4 %all-to-all-start.1 = ((bf16[64,24,1024]{2,1,0:T(8,128)(2,1)}), bf16[64,24,1024]{2,1,0:T(8,128)(2,1)}, u32[]{:S(2)}, u32[]{:S(2)}) async-start(bf16[64,24,1024]{2,1,0:T(8,128)(2,1)} %bitcast.25), calls=%async_computation.1 | async-start | bytes 6291456 | tf_op jit(solution)/shard_map/all_to_all | solution.py:383
  130.2 0.8 copy-start.8
  131.0 0.8 copy-start.10
  131.8 1.4 copy-start.2
  133.2 13.6 %copy-start.4 = (bf16[192,1536]{1,0:T(8,128)(2,1)}, bf16[192,1536]{1,0:T(8,128)(2,1)S(1)}, u32[]{:S(2)}) copy-start(bf16[192,1536]{1,0:T(8,128)(2,1)S(1)} %get-tuple-element.76.mask_ref) | copy-start | bytes 1769476
  133.2 13.6 %copy-start.6 = (bf16[192,1536]{1,0:T(8,128)(2,1)}, bf16[192,1536]{1,0:T(8,128)(2,1)S(1)}, u32[]{:S(2)}) copy-start(bf16[192,1536]{1,0:T(8,128)(2,1)S(1)} %get-tuple-element.68.high_ref) | copy-start | bytes 1769476
  170.3 5.3 %copy-start.13 = (f32[64,128]{1,0:T(8,128)S(1)}, f32[64,128]{1,0:T(8,128)}, u32[]{:S(2)}) copy-start(f32[64,128]{1,0:T(8,128)} %get-tuple-element.46.expert_ref) | copy-start | bytes 98308
  170.3 48.4 %all-to-all-start.2 = ((bf16[64,24,1024]{2,1,0:T(8,128)(2,1)}), bf16[64,24,1024]{2,1,0:T(8,128)(2,1)S(1)}, u32[]{:S(2)}, u32[]{:S(2)}) async-start(bf16[64,24,1024]{2,1,0:T(8,128)(2,1)} %bitcast.27), calls=%async_computation.2 | async-start | bytes 6291456 | tf_op jit(solution)/shard_map/all_to_all | solution.py:383
  175.5 1.1 copy-start.7
  176.6 1.1 copy-start.9
  177.7 1.0 copy-start.11
  183.9 41.7 %collective-permute-start = (bf16[48,1152]{1,0:T(8,128)(2,1)}, bf16[48,1152]{1,0:T(8,128)(2,1)}, u32[]{:S(2)}, u32[]{:S(2)}) collective-permute-start(bf16[48,1152]{1,0:T(8,128)(2,1)} %get-tuple-element.72), channel_id=1, source_target_pairs={{0,16},{8,24},{16,0},{24,8},{1,17},{9,25},{17,1},{25,9},{2,18},{10... | collective-permute-start | bytes 331784 | tf_op jit(solution)/shard_map/ppermute | solution.py:354
  186.6 42.6 %collective-permute-start.1 = (bf16[48,1152]{1,0:T(8,128)(2,1)}, bf16[48,1152]{1,0:T(8,128)(2,1)}, u32[]{:S(2)}, u32[]{:S(2)}) collective-permute-start(bf16[48,1152]{1,0:T(8,128)(2,1)} %get-tuple-element.73), channel_id=1, source_target_pairs={{0,8},{8,16},{16,24},{24,0},{1,9},{9,17},{17,25},{25,1},{2,10},{10... | collective-permute-start | bytes 331784 | tf_op jit(solution)/shard_map/ppermute | solution.py:354
  186.7 42.5 %collective-permute-start.2 = (bf16[48,1152]{1,0:T(8,128)(2,1)S(1)}, bf16[48,1152]{1,0:T(8,128)(2,1)}, u32[]{:S(2)}, u32[]{:S(2)}) collective-permute-start(bf16[48,1152]{1,0:T(8,128)(2,1)S(1)} %get-tuple-element.74), channel_id=1, source_target_pairs={{0,24},{8,0},{16,8},{24,16},{1,25},{9,1},{17,9},{25,17},{2,26},{10... | collective-permute-start | bytes 331784 | tf_op jit(solution)/shard_map/ppermute | solution.py:354
  218.6 1.1 copy-start.5
  221.2 11.5 %collective-permute-start.3 = (bf16[48,1024]{1,0:T(8,128)(2,1)}, bf16[48,1024]{1,0:T(8,128)(2,1)S(1)}, u32[]{:S(2)}, u32[]{:S(2)}) collective-permute-start(bf16[48,1024]{1,0:T(8,128)(2,1)} %get-tuple-element.78), channel_id=1, source_target_pairs={{0,16},{8,24},{16,0},{24,8},{1,17},{9,25},{17,1},{25,9},{2,18},{10... | collective-permute-start | bytes 294920 | tf_op jit(solution)/shard_map/ppermute | solution.py:354
  225.6 9.8 %collective-permute-start.4 = (bf16[48,1024]{1,0:T(8,128)(2,1)}, bf16[48,1024]{1,0:T(8,128)(2,1)S(1)}, u32[]{:S(2)}, u32[]{:S(2)}) collective-permute-start(bf16[48,1024]{1,0:T(8,128)(2,1)} %get-tuple-element.79), channel_id=1, source_target_pairs={{0,8},{8,16},{16,24},{24,0},{1,9},{9,17},{17,25},{25,1},{2,10},{10... | collective-permute-start | bytes 294920 | tf_op jit(solution)/shard_map/ppermute | solution.py:354
  225.7 9.8 %collective-permute-start.5 = (bf16[48,1024]{1,0:T(8,128)(2,1)}, bf16[48,1024]{1,0:T(8,128)(2,1)S(1)}, u32[]{:S(2)}, u32[]{:S(2)}) collective-permute-start(bf16[48,1024]{1,0:T(8,128)(2,1)} %get-tuple-element.80), channel_id=1, source_target_pairs={{0,24},{8,0},{16,8},{24,16},{1,25},{9,1},{17,9},{25,17},{2,26},{10... | collective-permute-start | bytes 294920 | tf_op jit(solution)/shard_map/ppermute | solution.py:354
